TPU v7x, 512 devices: a whole 4x8x8 slice. The times are simulated.
512 devices in a mesh: row: 16 (over x_lo, z), col: 32 (over y, x_hi, core).
Axes of the slice: x: 4 (x_hi: 2, x_lo: 2; x = x_hi * 2 + x_lo), y: 8, z: 8, core: 2. Of those that a mesh axis runs over, the one named last changes fastest.
Arguments:
- activations: bfloat16 [512, 32768], P('row', 'col'), may hold values from -6 to 6
- conv_one: bfloat16 [3, 3, 64, 64], replicated, may hold values from -0.25 to 0.25
- bias_one: float32 [64], replicated, may hold values from -3 to 3
- conv_two: bfloat16 [3, 3, 64, 64], replicated, may hold values from -0.25 to 0.25
- bias_two: float32 [64], replicated, may hold values from -3 to 3
- cotangent: bfloat16 [512, 32768], P('row', 'col'), may hold values from -6 to 6
Outputs:
- symmetric_out: bfloat16 [512, 32768], P('row', 'col')
- input_grad: bfloat16 [512, 32768], P('row', 'col')
- grad_w1: float32 [3, 3, 64, 64], replicated
- grad_b1: float32 [64], replicated
- grad_w2: float32 [3, 3, 64, 64], replicated
- grad_b2: float32 [64], replicated
All inputs are finite; a program needn't handle non-finite values.
Results may differ from a plain program's by a relative error of at most 0.01.
Values may be sent and summed in bfloat16 or wider, within the bound.
A program may use at most 64 MiB of HBM per device.

v0:
```python
import jax
import jax.numpy as jnp
from jax import lax
from jax.sharding import PartitionSpec as P

DILATION = 4


def padded_2(cells, sides, width):
    for axis, dim in sides:
        count = lax.axis_size(axis)
        ends = count - 1
        head = lax.slice_in_dim(cells, 0, width, axis=dim)
        tail = lax.slice_in_dim(cells, cells.shape[dim] - width, cells.shape[dim], axis=dim)
        cells = jnp.concatenate(
            [
                lax.ppermute(tail, axis, [(i, (i + 1) % count) for i in range(ends)]),
                cells,
                lax.ppermute(head, axis, [((i + 1) % count, i) for i in range(ends)]),
            ],
            axis=dim,
        )
    return cells


def activate(values):
    return jax.nn.gelu(values, approximate=True)


def dilated(padded, kernel):
    return lax.conv_general_dilated(
        padded[None],
        kernel,
        (1, 1),
        "VALID",
        rhs_dilation=(DILATION, DILATION),
        dimension_numbers=("NHWC", "HWIO", "NHWC"),
        preferred_element_type=jnp.float32,
    )[0]


def flipped(kernel):
    return jnp.swapaxes(kernel[::-1, ::-1], 2, 3)


def kernel_grad(padded, out_grad):
    row_count, col_count, channels = out_grad.shape
    rows_out = []
    for tap_row in range(3):
        cols_out = []
        for tap_col in range(3):
            window = lax.slice(
                padded,
                (tap_row * DILATION, tap_col * DILATION, 0),
                (tap_row * DILATION + row_count, tap_col * DILATION + col_count, padded.shape[2]),
            )
            cols_out.append(
                jnp.einsum("rci,rco->io", window, out_grad, preferred_element_type=jnp.float32)
            )
        rows_out.append(jnp.stack(cols_out))
    return jnp.stack(rows_out)


def mirror_tile(patch_in):
    col_total = lax.axis_size("col")
    row_total = lax.axis_size("row")
    fold_ratio = col_total // row_total
    row_count, col_count, channels = patch_in.shape
    blocks = patch_in.reshape(fold_ratio, col_count * col_count * channels)
    sectioned = blocks.reshape(fold_ratio, col_total, -1)
    sectioned = lax.all_to_all(
        lax.all_to_all(sectioned, "col", split_axis=1, concat_axis=1, tiled=True),
        "row",
        split_axis=1,
        concat_axis=0,
        tiled=True,
    )
    sectioned = lax.all_to_all(sectioned, "col", split_axis=0, concat_axis=0, tiled=True)
    mirrored = jnp.swapaxes(sectioned, 0, 1)
    mirrored = mirrored.reshape(fold_ratio, col_count, col_count, channels)
    return jnp.swapaxes(mirrored, 1, 2).reshape(row_count, col_count, channels)


def symmetric(patch_in):
    values = patch_in.astype(jnp.float32) + mirror_tile(patch_in).astype(jnp.float32)
    return (values * 0.5).astype(jnp.bfloat16)


def on_device(activations, conv_one, bias_one, conv_two, bias_two, cotangent):
    channels = conv_one.shape[2]
    row_count = activations.shape[0]
    col_count = activations.shape[1] // channels
    source = activations.reshape(row_count, col_count, channels)
    padded_in = padded_2(source, (("row", 0), ("col", 1)), DILATION)
    preact = dilated(padded_in, conv_one) + bias_one
    hidden = activate(preact).astype(jnp.bfloat16)
    hidden_pad = padded_2(hidden, (("row", 0), ("col", 1)), DILATION)
    branch = dilated(hidden_pad, conv_two) + bias_two
    summed = (source.astype(jnp.float32) + branch).astype(jnp.bfloat16)
    symmetric_out = symmetric(summed)
    sym_grad = symmetric(cotangent.reshape(row_count, col_count, channels))
    grad_pad = padded_2(sym_grad, (("row", 0), ("col", 1)), DILATION)
    hid_grad = dilated(grad_pad, flipped(conv_two))
    pre_grad = jax.vjp(activate, preact)[1](hid_grad)[0].astype(jnp.bfloat16)
    pre_pad = padded_2(pre_grad, (("row", 0), ("col", 1)), DILATION)
    input_grad = (sym_grad.astype(jnp.float32) + dilated(pre_pad, flipped(conv_one))).astype(
        jnp.bfloat16
    )
    inv_bins = 1.0 / (row_count * lax.axis_size("row"))
    totals = lax.psum(
        (
            kernel_grad(padded_in, pre_grad) * inv_bins,
            jnp.sum(pre_grad, axis=(0, 1), dtype=jnp.float32) * inv_bins,
            kernel_grad(hidden_pad, sym_grad) * inv_bins,
            jnp.sum(sym_grad, axis=(0, 1), dtype=jnp.float32) * inv_bins,
        ),
        ("row", "col"),
    )
    return (
        symmetric_out.reshape(row_count, col_count * channels),
        input_grad.reshape(row_count, col_count * channels),
        totals[0],
        totals[1],
        totals[2],
        totals[3],
    )


def solution(mesh):
    return jax.shard_map(
        on_device,
        mesh=mesh,
        in_specs=(P("row", "col"), P(), P(), P(), P(), P("row", "col")),
        out_specs=(P("row", "col"), P("row", "col"), P(), P(), P(), P()),
        check_vma=False,
    )
```

profile of v0, /device:TPU:1, one launch (start us, length us, event | category | flops | bytes accessed | tf_op | source)
XLA Modules:
  0.0 439.6 jit_solution(1785318963793155892)
XLA Ops:
  7.2 0.9 reshape_reshape_reshape.3
  8.1 0.7 copy.183
  8.8 11.4 %all-to-all-start.3 = ((bf16[2,32,512]{2,0,1:T(2,128)(2,1)}), bf16[2,32,512]{2,0,1:T(2,128)(2,1)}, u32[]{:S(2)}, u32[]{:S(2)}) async-start(bf16[2,32,512]{2,0,1:T(2,128)(2,1)} %copy.183), calls=%async_computation.3 | async-start | bytes 131072 | tf_op jit(solution)/shard_map/all_to_all | solution.py:72
  20.3 4.0 collective-permute-start
  24.4 1.3 collective-permute-start.1
  25.9 4.2 all-to-all-done.3
  30.1 10.2 %all-to-all-start.4 = ((bf16[2,32,512]{2,0,1:T(2,128)(2,1)}), bf16[2,32,512]{2,0,1:T(2,128)(2,1)S(1)}, u32[]{:S(2)}, u32[]{:S(2)}) async-start(bf16[2,32,512]{2,0,1:T(2,128)(2,1)} %all-to-all-done.3), calls=%async_computation.4 | async-start | bytes 131072 | tf_op jit(solution)/shard_map/all_to_all | solution.py:71
  40.3 4.0 collective-permute-start.2
  44.3 1.9 collective-permute-start.3
  46.2 1.4 all-to-all-done.4
  47.6 0.7 copy.184
  48.3 9.5 %all-to-all-start.5 = ((bf16[32,2,512]{2,1,0:T(2,128)(2,1)}), bf16[32,2,512]{2,1,0:T(2,128)(2,1)S(1)}, u32[]{:S(2)}, u32[]{:S(2)}) async-start(bf16[32,2,512]{2,1,0:T(2,128)(2,1)} %bitcast.10), calls=%async_computation.5 | async-start | bytes 131072 | tf_op jit(solution)/shard_map/all_to_all | solution.py:78
  59.0 8.7 %all-to-all-done.5 = bf16[32,2,512]{2,1,0:T(2,128)(2,1)S(1)} async-done(((bf16[32,2,512]{2,1,0:T(2,128)(2,1)}), bf16[32,2,512]{2,1,0:T(2,128)(2,1)S(1)}, u32[]{:S(2)}, u32[]{:S(2)}) %all-to-all-start.5) | async-done | bytes 65568 | tf_op jit(solution)/shard_map/all_to_all | solution.py:78
  68.0 2.6 collective-permute-start.8
  70.7 1.3 collective-permute-start.9
  72.0 1.0 fusion
  73.0 2.2 collective-permute-done.9
  75.2 4.5 %collective-permute-start.10 = (bf16[40,4,64]{2,1,0:T(4,128)(2,1)S(1)}, bf16[40,4,64]{2,1,0:T(4,128)(2,1)S(1)}, u32[]{:S(2)}, u32[]{:S(2)}) collective-permute-start(bf16[40,4,64]{2,1,0:T(4,128)(2,1)S(1)} %get-tuple-element.21), channel_id=1, source_target_pairs={{0,1},{1,2},{2,3},{3,4},{4,5},{5,6},{6,7},{7,8},{8,9},{9,10},{10,1... | collective-permute-start | bytes 61448 | tf_op jit(solution)/shard_map/ppermute | solution.py:17
  79.7 1.9 collective-permute-start.11
  81.9 4.7 %collective-permute-done.11 = bf16[40,4,64]{2,1,0:T(4,128)(2,1)S(1)} collective-permute-done((bf16[40,4,64]{2,1,0:T(4,128)(2,1)S(1)}, bf16[40,4,64]{2,1,0:T(4,128)(2,1)S(1)}, u32[]{:S(2)}, u32[]{:S(2)}) %collective-permute-start.11) | collective-permute-done | bytes 20512 | tf_op jit(solution)/shard_map/ppermute | solution.py:19
  86.7 2.1 fusion.3
  88.8 0.6 copy-done.5
  91.4 2.6 collective-permute-start.12
  94.1 1.3 collective-permute-start.13
  95.4 4.4 collective-permute-start.4
  99.8 1.3 collective-permute-start.5
  101.6 0.7 maximum_multiply_fusion
  102.4 2.5 collective-permute-start.14
  104.8 1.9 collective-permute-start.15
  106.8 5.1 %collective-permute-start.6 = (bf16[40,4,64]{2,1,0:T(4,128)(2,1)S(1)}, bf16[40,4,64]{2,1,0:T(4,128)(2,1)S(1)}, u32[]{:S(2)}, u32[]{:S(2)}) collective-permute-start(bf16[40,4,64]{2,1,0:T(4,128)(2,1)S(1)} %get-tuple-element.23), channel_id=1, source_target_pairs={{0,1},{1,2},{2,3},{3,4},{4,5},{5,6},{6,7},{7,8},{8,9},{9,10},{10,1... | collective-permute-start | bytes 61448 | tf_op jit(solution)/shard_map/ppermute | solution.py:17
  112.0 2.1 collective-permute-start.7
  114.5 4.3 collective-permute-done.7
  120.1 2.7 convolution_reduce_fusion
  123.6 2.2 fusion.54
  126.0 0.7 copy.179
  126.7 10.9 %all-to-all-start = ((bf16[2,32,512]{2,0,1:T(2,128)(2,1)}), bf16[2,32,512]{2,0,1:T(2,128)(2,1)}, u32[]{:S(2)}, u32[]{:S(2)}) async-start(bf16[2,32,512]{2,0,1:T(2,128)(2,1)} %copy.179), calls=%async_computation | async-start | bytes 131072 | tf_op jit(solution)/shard_map/all_to_all | solution.py:72
  137.6 0.7 convert_reduce_fusion.1
  138.4 9.0 %all-to-all-done = bf16[2,32,512]{2,0,1:T(2,128)(2,1)} async-done(((bf16[2,32,512]{2,0,1:T(2,128)(2,1)}), bf16[2,32,512]{2,0,1:T(2,128)(2,1)}, u32[]{:S(2)}, u32[]{:S(2)}) %all-to-all-start) | async-done | bytes 65568 | tf_op jit(solution)/shard_map/all_to_all | solution.py:72
  147.4 10.0 %all-to-all-start.1 = ((bf16[2,32,512]{2,0,1:T(2,128)(2,1)}), bf16[2,32,512]{2,0,1:T(2,128)(2,1)S(1)}, u32[]{:S(2)}, u32[]{:S(2)}) async-start(bf16[2,32,512]{2,0,1:T(2,128)(2,1)} %all-to-all-done), calls=%async_computation.1 | async-start | bytes 131072 | tf_op jit(solution)/shard_map/all_to_all | solution.py:71
  157.8 0.7 maximum_multiply_fusion.1
  158.5 6.3 %all-to-all-done.1 = bf16[2,32,512]{2,0,1:T(2,128)(2,1)S(1)} async-done(((bf16[2,32,512]{2,0,1:T(2,128)(2,1)}), bf16[2,32,512]{2,0,1:T(2,128)(2,1)S(1)}, u32[]{:S(2)}, u32[]{:S(2)}) %all-to-all-start.1) | async-done | bytes 65568 | tf_op jit(solution)/shard_map/all_to_all | solution.py:71
  164.8 0.7 copy.180
  165.5 5.3 %all-to-all-start.2 = ((bf16[32,2,512]{2,1,0:T(2,128)(2,1)}), bf16[32,2,512]{2,1,0:T(2,128)(2,1)S(1)}, u32[]{:S(2)}, u32[]{:S(2)}) async-start(bf16[32,2,512]{2,1,0:T(2,128)(2,1)} %bitcast.5), calls=%async_computation.2 | async-start | bytes 131072 | tf_op jit(solution)/shard_map/all_to_all | solution.py:78
  170.9 98.1 %all-reduce = (f32[64]{0:T(128)}, f32[64]{0:T(128)}) all-reduce(f32[64]{0:T(128)S(1)} %broadcast_multiply_fusion.1, f32[64]{0:T(128)S(1)} %broadcast_multiply_fusion), channel_id=1, replica_groups=mesh['row'=16,'col'=32] {'row','col'}, use_global_device_ids=true, to_apply=%region_2.0 | all-reduce | flops 128 | bytes 1024 | tf_op jit(solution)/shard_map/psum | solution.py:110
  269.4 0.7 multiply_convert_fusion.2
  270.0 160.3 %all-reduce.4.cloned.1.call-done = (f32[3,3,64,64]{3,2,1,0:T(8,128)}, f32[3,3,64,64]{3,2,1,0:T(8,128)}) async-done(((f32[3,3,64,64]{3,2,1,0:T(8,128)}, f32[3,3,64,64]{3,2,1,0:T(8,128)}), (f32[3,3,64,64]{3,2,1,0:T(8,128)}, f32[3,3,64,64]{3,2,1,0:T(8,128)})) %all-reduce.4.cloned.1.call-update) | async-done | bytes 294928 | tf_op jit(solution)/shard_map/psum | solution.py:110
  430.3 1.7 copy.233
  432.1 0.7 copy.234
  (98 shorter events, 8.2 us)
Async XLA Ops:
  7.2 79.5 %copy-start = (bf16[3,3,64,64]{3,2,1,0:T(8,128)(2,1)S(1)}, bf16[3,3,64,64]{3,2,1,0:T(8,128)(2,1)}, u32[]{:S(2)}) copy-start(bf16[3,3,64,64]{3,2,1,0:T(8,128)(2,1)} %param.9) | copy-start | bytes 221188
  8.8 11.4 %copy-start.1 = (bf16[32,1024]{1,0:T(8,128)(2,1)S(1)}, bf16[32,1024]{1,0:T(8,128)(2,1)}, u32[]{:S(2)}) copy-start(bf16[32,1024]{1,0:T(8,128)(2,1)} %param.6) | copy-start | bytes 196612
  8.8 21.3 %all-to-all-start.3 = ((bf16[2,32,512]{2,0,1:T(2,128)(2,1)}), bf16[2,32,512]{2,0,1:T(2,128)(2,1)}, u32[]{:S(2)}, u32[]{:S(2)}) async-start(bf16[2,32,512]{2,0,1:T(2,128)(2,1)} %copy.183), calls=%async_computation.3 | async-start | bytes 131072 | tf_op jit(solution)/shard_map/all_to_all | solution.py:72
  20.3 19.9 %collective-permute-start = (bf16[4,16,64]{2,0,1:T(4,128)(2,1)S(1)}, bf16[4,16,64]{2,0,1:T(4,128)(2,1)S(1)}, u32[]{:S(2)}, u32[]{:S(2)}) collective-permute-start(bf16[4,16,64]{2,0,1:T(4,128)(2,1)S(1)} %copy.173), channel_id=1, source_target_pairs={{0,32},{32,64},{64,96},{96,128},{128,160},{160,192},{192,224},{224... | collective-permute-start | bytes 24584 | tf_op jit(solution)/shard_map/ppermute | solution.py:17
  24.4 15.8 %collective-permute-start.1 = (bf16[4,16,64]{2,0,1:T(4,128)(2,1)S(1)}, bf16[4,16,64]{2,0,1:T(4,128)(2,1)S(1)}, u32[]{:S(2)}, u32[]{:S(2)}) collective-permute-start(bf16[4,16,64]{2,0,1:T(4,128)(2,1)S(1)} %copy.174), channel_id=1, source_target_pairs={{32,0},{64,32},{96,64},{128,96},{160,128},{192,160},{224,192},{256... | collective-permute-start | bytes 24584 | tf_op jit(solution)/shard_map/ppermute | solution.py:19
  30.1 17.5 %all-to-all-start.4 = ((bf16[2,32,512]{2,0,1:T(2,128)(2,1)}), bf16[2,32,512]{2,0,1:T(2,128)(2,1)S(1)}, u32[]{:S(2)}, u32[]{:S(2)}) async-start(bf16[2,32,512]{2,0,1:T(2,128)(2,1)} %all-to-all-done.3), calls=%async_computation.4 | async-start | bytes 131072 | tf_op jit(solution)/shard_map/all_to_all | solution.py:71
  40.3 18.5 %collective-permute-start.2 = (bf16[40,4,64]{2,0,1:T(8,128)(2,1)S(1)}, bf16[40,4,64]{2,0,1:T(8,128)(2,1)S(1)}, u32[]{:S(2)}, u32[]{:S(2)}) collective-permute-start(bf16[40,4,64]{2,0,1:T(8,128)(2,1)S(1)} %get-tuple-element.25), channel_id=1, source_target_pairs={{0,1},{1,2},{2,3},{3,4},{4,5},{5,6},{6,7},{7,8},{8,9},{9,10},{10,1... | collective-permute-start | bytes 61448 | tf_op jit(solution)/shard_map/ppermute | solution.py:17
  44.3 14.6 %collective-permute-start.3 = (bf16[40,4,64]{2,0,1:T(8,128)(2,1)S(1)}, bf16[40,4,64]{2,0,1:T(8,128)(2,1)S(1)}, u32[]{:S(2)}, u32[]{:S(2)}) collective-permute-start(bf16[40,4,64]{2,0,1:T(8,128)(2,1)S(1)} %get-tuple-element.26), channel_id=1, source_target_pairs={{1,0},{2,1},{3,2},{4,3},{5,4},{6,5},{7,6},{8,7},{9,8},{10,9},{11,1... | collective-permute-start | bytes 61448 | tf_op jit(solution)/shard_map/ppermute | solution.py:19
  48.3 9.6 %copy-start.2 = (bf16[32,1024]{1,0:T(8,128)(2,1)S(1)}, bf16[32,1024]{1,0:T(8,128)(2,1)}, u32[]{:S(2)}) copy-start(bf16[32,1024]{1,0:T(8,128)(2,1)} %param.11) | copy-start | bytes 196612
  48.3 19.4 %all-to-all-start.5 = ((bf16[32,2,512]{2,1,0:T(2,128)(2,1)}), bf16[32,2,512]{2,1,0:T(2,128)(2,1)S(1)}, u32[]{:S(2)}, u32[]{:S(2)}) async-start(bf16[32,2,512]{2,1,0:T(2,128)(2,1)} %bitcast.10), calls=%async_computation.5 | async-start | bytes 131072 | tf_op jit(solution)/shard_map/all_to_all | solution.py:78
  58.0 0.7 copy-start.4
  68.0 4.0 copy-start.6
  68.0 4.9 %collective-permute-start.8 = (bf16[4,16,64]{2,1,0:T(8,128)(2,1)S(1)}, bf16[4,16,64]{2,1,0:T(8,128)(2,1)S(1)}, u32[]{:S(2)}, u32[]{:S(2)}) collective-permute-start(bf16[4,16,64]{2,1,0:T(8,128)(2,1)S(1)} %get-tuple-element.29), channel_id=1, source_target_pairs={{0,32},{32,64},{64,96},{96,128},{128,160},{160,192},{192,224},{224... | collective-permute-start | bytes 24584 | tf_op jit(solution)/shard_map/ppermute | solution.py:17
  70.7 4.5 %collective-permute-start.9 = (bf16[4,16,64]{2,1,0:T(8,128)(2,1)S(1)}, bf16[4,16,64]{2,1,0:T(8,128)(2,1)S(1)}, u32[]{:S(2)}, u32[]{:S(2)}) collective-permute-start(bf16[4,16,64]{2,1,0:T(8,128)(2,1)S(1)} %get-tuple-element.30), channel_id=1, source_target_pairs={{32,0},{64,32},{96,64},{128,96},{160,128},{192,160},{224,192},{256... | collective-permute-start | bytes 24584 | tf_op jit(solution)/shard_map/ppermute | solution.py:19
  75.2 6.7 %collective-permute-start.10 = (bf16[40,4,64]{2,1,0:T(4,128)(2,1)S(1)}, bf16[40,4,64]{2,1,0:T(4,128)(2,1)S(1)}, u32[]{:S(2)}, u32[]{:S(2)}) collective-permute-start(bf16[40,4,64]{2,1,0:T(4,128)(2,1)S(1)} %get-tuple-element.21), channel_id=1, source_target_pairs={{0,1},{1,2},{2,3},{3,4},{4,5},{5,6},{6,7},{7,8},{8,9},{9,10},{10,1... | collective-permute-start | bytes 61448 | tf_op jit(solution)/shard_map/ppermute | solution.py:17
  79.7 6.8 %collective-permute-start.11 = (bf16[40,4,64]{2,1,0:T(4,128)(2,1)S(1)}, bf16[40,4,64]{2,1,0:T(4,128)(2,1)S(1)}, u32[]{:S(2)}, u32[]{:S(2)}) collective-permute-start(bf16[40,4,64]{2,1,0:T(4,128)(2,1)S(1)} %get-tuple-element.22), channel_id=1, source_target_pairs={{1,0},{2,1},{3,2},{4,3},{5,4},{6,5},{7,6},{8,7},{9,8},{10,9},{11,1... | collective-permute-start | bytes 61448 | tf_op jit(solution)/shard_map/ppermute | solution.py:19
  88.8 0.7 copy-start.5
  91.4 10.9 %collective-permute-start.12 = (bf16[4,16,64]{2,1,0:T(8,128)(2,1)S(1)}, bf16[4,16,64]{2,1,0:T(8,128)(2,1)S(1)}, u32[]{:S(2)}, u32[]{:S(2)}) collective-permute-start(bf16[4,16,64]{2,1,0:T(8,128)(2,1)S(1)} %get-tuple-element.27), channel_id=1, source_target_pairs={{0,32},{32,64},{64,96},{96,128},{128,160},{160,192},{192,224},{224... | collective-permute-start | bytes 24584 | tf_op jit(solution)/shard_map/ppermute | solution.py:17
  94.1 8.3 %collective-permute-start.13 = (bf16[4,16,64]{2,1,0:T(8,128)(2,1)S(1)}, bf16[4,16,64]{2,1,0:T(8,128)(2,1)S(1)}, u32[]{:S(2)}, u32[]{:S(2)}) collective-permute-start(bf16[4,16,64]{2,1,0:T(8,128)(2,1)S(1)} %get-tuple-element.28), channel_id=1, source_target_pairs={{32,0},{64,32},{96,64},{128,96},{160,128},{192,160},{224,192},{256... | collective-permute-start | bytes 24584 | tf_op jit(solution)/shard_map/ppermute | solution.py:19
  95.4 11.4 %collective-permute-start.4 = (bf16[4,16,64]{2,1,0:T(8,128)(2,1)S(1)}, bf16[4,16,64]{2,1,0:T(8,128)(2,1)S(1)}, u32[]{:S(2)}, u32[]{:S(2)}) collective-permute-start(bf16[4,16,64]{2,1,0:T(8,128)(2,1)S(1)} %get-tuple-element.31), channel_id=1, source_target_pairs={{0,32},{32,64},{64,96},{96,128},{128,160},{160,192},{192,224},{224... | collective-permute-start | bytes 24584 | tf_op jit(solution)/shard_map/ppermute | solution.py:17
  99.8 7.0 %collective-permute-start.5 = (bf16[4,16,64]{2,1,0:T(8,128)(2,1)S(1)}, bf16[4,16,64]{2,1,0:T(8,128)(2,1)S(1)}, u32[]{:S(2)}, u32[]{:S(2)}) collective-permute-start(bf16[4,16,64]{2,1,0:T(8,128)(2,1)S(1)} %get-tuple-element.32), channel_id=1, source_target_pairs={{32,0},{64,32},{96,64},{128,96},{160,128},{192,160},{224,192},{256... | collective-permute-start | bytes 24584 | tf_op jit(solution)/shard_map/ppermute | solution.py:19
  102.4 17.6 %collective-permute-start.14 = (bf16[40,4,64]{2,1,0:T(4,128)(2,1)S(1)}, bf16[40,4,64]{2,1,0:T(4,128)(2,1)S(1)}, u32[]{:S(2)}, u32[]{:S(2)}) collective-permute-start(bf16[40,4,64]{2,1,0:T(4,128)(2,1)S(1)} %get-tuple-element.19), channel_id=1, source_target_pairs={{0,1},{1,2},{2,3},{3,4},{4,5},{5,6},{6,7},{7,8},{8,9},{9,10},{10,1... | collective-permute-start | bytes 61448 | tf_op jit(solution)/shard_map/ppermute | solution.py:17
  104.8 15.2 %collective-permute-start.15 = (bf16[40,4,64]{2,1,0:T(4,128)(2,1)S(1)}, bf16[40,4,64]{2,1,0:T(4,128)(2,1)S(1)}, u32[]{:S(2)}, u32[]{:S(2)}) collective-permute-start(bf16[40,4,64]{2,1,0:T(4,128)(2,1)S(1)} %get-tuple-element.20), channel_id=1, source_target_pairs={{1,0},{2,1},{3,2},{4,3},{5,4},{6,5},{7,6},{8,7},{9,8},{10,9},{11,1... | collective-permute-start | bytes 61448 | tf_op jit(solution)/shard_map/ppermute | solution.py:19
  106.8 7.7 %collective-permute-start.6 = (bf16[40,4,64]{2,1,0:T(4,128)(2,1)S(1)}, bf16[40,4,64]{2,1,0:T(4,128)(2,1)S(1)}, u32[]{:S(2)}, u32[]{:S(2)}) collective-permute-start(bf16[40,4,64]{2,1,0:T(4,128)(2,1)S(1)} %get-tuple-element.23), channel_id=1, source_target_pairs={{0,1},{1,2},{2,3},{3,4},{4,5},{5,6},{6,7},{7,8},{8,9},{9,10},{10,1... | collective-permute-start | bytes 61448 | tf_op jit(solution)/shard_map/ppermute | solution.py:17
  112.0 6.8 %collective-permute-start.7 = (bf16[40,4,64]{2,1,0:T(4,128)(2,1)S(1)}, bf16[40,4,64]{2,1,0:T(4,128)(2,1)S(1)}, u32[]{:S(2)}, u32[]{:S(2)}) collective-permute-start(bf16[40,4,64]{2,1,0:T(4,128)(2,1)S(1)} %get-tuple-element.24), channel_id=1, source_target_pairs={{1,0},{2,1},{3,2},{4,3},{5,4},{6,5},{7,6},{8,7},{9,8},{10,9},{11,1... | collective-permute-start | bytes 61448 | tf_op jit(solution)/shard_map/ppermute | solution.py:19
  126.7 20.8 %all-to-all-start = ((bf16[2,32,512]{2,0,1:T(2,128)(2,1)}), bf16[2,32,512]{2,0,1:T(2,128)(2,1)}, u32[]{:S(2)}, u32[]{:S(2)}) async-start(bf16[2,32,512]{2,0,1:T(2,128)(2,1)} %copy.179), calls=%async_computation | async-start | bytes 131072 | tf_op jit(solution)/shard_map/all_to_all | solution.py:72
  147.4 17.4 %all-to-all-start.1 = ((bf16[2,32,512]{2,0,1:T(2,128)(2,1)}), bf16[2,32,512]{2,0,1:T(2,128)(2,1)S(1)}, u32[]{:S(2)}, u32[]{:S(2)}) async-start(bf16[2,32,512]{2,0,1:T(2,128)(2,1)} %all-to-all-done), calls=%async_computation.1 | async-start | bytes 131072 | tf_op jit(solution)/shard_map/all_to_all | solution.py:71
  157.5 272.9 %all-reduce.4.cloned.1.call-start = ((), (), s32[]{:S(2)}) async-start(), calls=%async_computation.6 | async-start | bytes 1179648 | tf_op jit(solution)/shard_map/psum | solution.py:110
  165.5 103.5 %all-to-all-start.2 = ((bf16[32,2,512]{2,1,0:T(2,128)(2,1)}), bf16[32,2,512]{2,1,0:T(2,128)(2,1)S(1)}, u32[]{:S(2)}, u32[]{:S(2)}) async-start(bf16[32,2,512]{2,1,0:T(2,128)(2,1)} %bitcast.5), calls=%async_computation.2 | async-start | bytes 131072 | tf_op jit(solution)/shard_map/all_to_all | solution.py:78
  430.3 1.7 copy-start.3
Sparse Core Ops, SparseCore 0:
  164.1 266.2 all-reduce.3
where the time goes:
time: 441 us; the launch traced here: 440 us
  waiting for transfers between devices  201 us (46%)
  starting transfers between devices  100 us (23%)
  blocking collectives  98.1 us (22%)
  between operations  14.7 us (3%)
  matrix products  11.6 us (3%)
  local copies, waits for them, and re-layouts  9.79 us (2%)
    psum x1, waiting for transfers between devices, on_device(): lax.psum((kernel_grad(padded_in, pre_grad) * inv_bins, jnp.sum(pre_grad,...  160 us
    psum x1, blocking collectives, on_device(): lax.psum((kernel_grad(padded_in, pre_grad) * inv_bins, jnp.sum(pre_grad,...  98.1 us
    ppermute x8, starting transfers between devices, padded_2(): lax.ppermute(tail, axis, [(i, (i + 1) % count) for i in range(ends)])  29.8 us
    all_to_all x2, starting transfers between devices, mirror_tile(): lax.all_to_all(sectioned, 'col', split_axis=1, concat_axis=1, tiled=True)  22.3 us
    all_to_all x2, starting transfers between devices, mirror_tile(): lax.all_to_all(lax.all_to_all(sectioned, 'col', split_axis=1, concat_axis...  20.2 us
    all_to_all x2, starting transfers between devices, mirror_tile(): lax.all_to_all(sectioned, 'col', split_axis=0, concat_axis=0, tiled=True)  14.9 us
    all_to_all x2, waiting for transfers between devices, mirror_tile(): lax.all_to_all(sectioned, 'col', split_axis=1, concat_axis=1, tiled=True)  13.1 us
    ppermute x8, starting transfers between devices, padded_2(): lax.ppermute(head, axis, [((i + 1) % count, i) for i in range(ends)])  13 us
  transfers between devices with their start and end apart: 23, of which 9 were waited for; matrix products, arithmetic and copies ran while one was open for 2% of the time, Pallas kernels for 0%

commit v1 on v0

--- a/solution.py
+++ b/solution.py
@@ -1,9 +1,167 @@
 import jax
 import jax.numpy as jnp
 from jax import lax
+from jax.experimental import pallas as pl
+from jax.experimental.pallas import tpu as pltpu
 from jax.sharding import PartitionSpec as P
 
 DILATION = 4
+MESH = pl.DeviceIdType.MESH
+WIDE = 8
+PLANE = 64
+OWNERS = 10
+ROWS = 72
+PIECE = 80
+
+
+def place():
+    row = lax.axis_index("row")
+    col = lax.axis_index("col")
+    near = lax.rem(col, 4) * 2 + row // 8
+    far = (col // 4) * 8 + lax.rem(row, 8)
+    return row, col, near, far
+
+
+def near_id(row, col, peer):
+    return (lax.rem(peer, 2) * 8 + lax.rem(row, 8), (col // 4) * 4 + peer // 2)
+
+
+def far_id(row, col, peer):
+    return ((row // 8) * 8 + lax.rem(peer, 8), (peer // 8) * 4 + lax.rem(col, 4))
+
+
+def reduce_kernel(parts, full, got_a, mine, got_b, total, a_send, a_recv, b_send, b_recv, t_send, t_recv, c_send, c_recv):
+    row, col, near, far = place()
+    lead = far - near
+    owned = lead // 6
+    is_owner = (lead >= 0) & (lax.rem(lead, 6) == 0) & (owned < OWNERS)
+
+    barrier = pltpu.get_barrier_semaphore()
+    for step in range(1, WIDE):
+        pl.semaphore_signal(barrier, inc=1, device_id=near_id(row, col, lax.rem(near + step, WIDE)), device_id_type=MESH)
+    for tile in range(OWNERS):
+        owner = 6 * tile + near
+
+        @pl.when(owner != far)
+        def _():
+            pl.semaphore_signal(barrier, inc=1, device_id=far_id(row, col, owner), device_id_type=MESH)
+
+    @pl.when(is_owner)
+    def _():
+        @pl.loop(1, PLANE)
+        def _(step):
+            pl.semaphore_signal(barrier, inc=1, device_id=far_id(row, col, lax.rem(far + step, PLANE)), device_id_type=MESH)
+
+    pl.semaphore_wait(barrier, WIDE - 1 + OWNERS + jnp.where(is_owner, PLANE - 2, 0))
+
+    sends = []
+    for step in range(1, WIDE):
+        peer = lax.rem(near + step, WIDE)
+        copy = pltpu.make_async_remote_copy(
+            src_ref=parts.at[peer],
+            dst_ref=got_a.at[step - 1],
+            send_sem=a_send.at[step - 1],
+            recv_sem=a_recv.at[step - 1],
+            device_id=near_id(row, col, peer),
+            device_id_type=MESH,
+        )
+        copy.start()
+        sends.append(copy)
+    acc = parts[near]
+    for step in range(1, WIDE):
+        sends[step - 1].wait_recv()
+        acc = acc + got_a[step - 1]
+    mine[...] = acc.reshape(OWNERS, 8, 128)
+
+    for tile in range(OWNERS):
+        owner = 6 * tile + near
+
+        @pl.when(owner != far)
+        def _():
+            pltpu.make_async_remote_copy(
+                src_ref=mine.at[tile],
+                dst_ref=got_b.at[far],
+                send_sem=b_send,
+                recv_sem=b_recv,
+                device_id=far_id(row, col, owner),
+                device_id_type=MESH,
+            ).start()
+
+    @pl.when(is_owner)
+    def _():
+        got_b[far] = mine[owned]
+        pltpu.make_async_copy(got_b.at[pl.ds(0, PLANE - 1)], got_b.at[pl.ds(0, PLANE - 1)], b_recv).wait()
+        total[owned] = jnp.sum(got_b[...], axis=0)
+
+        @pl.loop(1, PLANE)
+        def _(step):
+            pltpu.make_async_remote_copy(
+                src_ref=total.at[owned],
+                dst_ref=total.at[owned],
+                send_sem=t_send,
+                recv_sem=t_recv,
+                device_id=far_id(row, col, lax.rem(far + step, PLANE)),
+                device_id_type=MESH,
+            ).start()
+
+        pltpu.make_async_copy(total.at[pl.ds(0, OWNERS - 1)], total.at[pl.ds(0, OWNERS - 1)], t_recv).wait()
+
+    @pl.when(jnp.logical_not(is_owner))
+    def _():
+        pltpu.make_async_copy(total, total, t_recv).wait()
+
+    lasts = []
+    for step in range(1, WIDE):
+        peer = lax.rem(near + step, WIDE)
+        copy = pltpu.make_async_remote_copy(
+            src_ref=total,
+            dst_ref=full.at[near],
+            send_sem=c_send.at[step - 1],
+            recv_sem=c_recv.at[step - 1],
+            device_id=near_id(row, col, peer),
+            device_id_type=MESH,
+        )
+        copy.start()
+        lasts.append(copy)
+    full[near] = total[...]
+    for copy in sends:
+        copy.wait_send()
+
+    @pl.when(is_owner)
+    def _():
+        pltpu.make_async_copy(total.at[pl.ds(0, OWNERS - 1)], total.at[pl.ds(0, OWNERS - 1)], b_send).wait()
+        pltpu.make_async_copy(got_b.at[pl.ds(0, PLANE - 1)], got_b.at[pl.ds(0, PLANE - 1)], t_send).wait()
+
+    @pl.when(jnp.logical_not(is_owner))
+    def _():
+        pltpu.make_async_copy(total, total, b_send).wait()
+
+    for copy in lasts:
+        copy.wait()
+
+
+def reduce_all(parts):
+    return pl.pallas_call(
+        reduce_kernel,
+        out_shape=jax.ShapeDtypeStruct((WIDE, OWNERS, 8, 128), jnp.float32),
+        in_specs=[pl.BlockSpec(memory_space=pltpu.VMEM)],
+        out_specs=pl.BlockSpec(memory_space=pltpu.VMEM),
+        scratch_shapes=[
+            pltpu.VMEM((WIDE - 1, PIECE, 128), jnp.float32),
+            pltpu.VMEM((OWNERS, 8, 128), jnp.float32),
+            pltpu.VMEM((PLANE, 8, 128), jnp.float32),
+            pltpu.VMEM((OWNERS, 8, 128), jnp.float32),
+            pltpu.SemaphoreType.DMA((WIDE - 1,)),
+            pltpu.SemaphoreType.DMA((WIDE - 1,)),
+            pltpu.SemaphoreType.DMA,
+            pltpu.SemaphoreType.DMA,
+            pltpu.SemaphoreType.DMA,
+            pltpu.SemaphoreType.DMA,
+            pltpu.SemaphoreType.DMA((WIDE - 1,)),
+            pltpu.SemaphoreType.DMA((WIDE - 1,)),
+        ],
+        compiler_params=pltpu.CompilerParams(collective_id=0, has_side_effects=True),
+    )(parts)
 
 
 def padded_2(cells, sides, width):
@@ -107,14 +265,30 @@
         jnp.bfloat16
     )
     inv_bins = 1.0 / (row_count * lax.axis_size("row"))
-    totals = lax.psum(
-        (
-            kernel_grad(padded_in, pre_grad) * inv_bins,
-            jnp.sum(pre_grad, axis=(0, 1), dtype=jnp.float32) * inv_bins,
-            kernel_grad(hidden_pad, sym_grad) * inv_bins,
-            jnp.sum(sym_grad, axis=(0, 1), dtype=jnp.float32) * inv_bins,
-        ),
-        ("row", "col"),
+    taps = jnp.concatenate(
+        [
+            kernel_grad(padded_in, pre_grad).reshape(9 * channels, channels),
+            kernel_grad(hidden_pad, sym_grad).reshape(9 * channels, channels),
+        ],
+        axis=1,
+    )
+    biases = jnp.concatenate(
+        [
+            jnp.sum(pre_grad, axis=(0, 1), dtype=jnp.float32),
+            jnp.sum(sym_grad, axis=(0, 1), dtype=jnp.float32),
+        ]
+    )
+    parts = jnp.concatenate(
+        [taps.reshape(WIDE, ROWS, 128), jnp.broadcast_to(biases, (WIDE, 8, 128))], axis=1
+    )
+    full = reduce_all(parts * inv_bins).reshape(WIDE, PIECE, 128)
+    taps = full[:, :ROWS].reshape(3, 3, channels, 2 * channels)
+    biases = full[0, ROWS]
+    totals = (
+        taps[..., :channels],
+        biases[:channels],
+        taps[..., channels:],
+        biases[channels:],
     )
     return (
         symmetric_out.reshape(row_count, col_count * channels),

time: 441 us -> 204 us (0.46)
  waiting for transfers between devices: 201 us -> 44.7 us
  blocking collectives: 98.1 us -> 0 us
  Pallas kernels: 0 us -> 30.9 us
  between operations: 14.7 us -> 1.37 us
    psum x1 -> x0, waiting for transfers between devices: 160 us -> none  [on_device(): lax.psum((kernel_grad(padded_in, pre_grad) * inv_bins, jnp.sum(pre_grad,...]
    psum x1 -> x0, blocking collectives: 98.1 us -> none  [on_device(): lax.psum((kernel_grad(padded_in, pre_grad) * inv_bins, jnp.sum(pre_grad,...]
    pallas_call x0 -> x1, Pallas kernels: none -> 30.9 us  [reduce_all(): pl.pallas_call(reduce_kernel, out_shape=jax.ShapeDtypeStruct((WIDE, OWNER...]
    all_to_all x2, waiting for transfers between devices: 8.72 us -> 18.3 us  [mirror_tile(): lax.all_to_all(sectioned, 'col', split_axis=0, concat_axis=0, tiled=True)]
  transfers between devices with their start and end apart: 23 -> 22, of which waited for: 9 -> 8; matrix products, arithmetic and copies ran while one was open for 2% -> 6% of each run, Pallas kernels for 0% -> 0%
where the time goes in v1:
time: 204 us; the launch traced here: 203 us
  starting transfers between devices  101 us (50%)
  waiting for transfers between devices  44.7 us (22%)
  Pallas kernels  30.9 us (15%)
  matrix products  11.6 us (6%)
  local copies, waits for them, and re-layouts  10.6 us (5%)
  other arithmetic  3.08 us (2%)
    pallas_call x1, Pallas kernels, reduce_all(): pl.pallas_call(reduce_kernel, out_shape=jax.ShapeDtypeStruct((WIDE, OWNER...  30.9 us
    ppermute x8, starting transfers between devices, padded_2(): lax.ppermute(tail, axis, [(i, (i + 1) % count) for i in range(ends)])  29.8 us
    all_to_all x2, starting transfers between devices, mirror_tile(): lax.all_to_all(sectioned, 'col', split_axis=1, concat_axis=1, tiled=True)  22.9 us
    all_to_all x2, starting transfers between devices, mirror_tile(): lax.all_to_all(lax.all_to_all(sectioned, 'col', split_axis=1, concat_axis...  20.2 us
    all_to_all x2, waiting for transfers between devices, mirror_tile(): lax.all_to_all(sectioned, 'col', split_axis=0, concat_axis=0, tiled=True)  18.3 us
    all_to_all x2, starting transfers between devices, mirror_tile(): lax.all_to_all(sectioned, 'col', split_axis=0, concat_axis=0, tiled=True)  14.9 us
    ppermute x8, starting transfers between devices, padded_2(): lax.ppermute(head, axis, [((i + 1) % count, i) for i in range(ends)])  12.9 us
    all_to_all x2, waiting for transfers between devices, mirror_tile(): lax.all_to_all(sectioned, 'col', split_axis=1, concat_axis=1, tiled=True)  11 us
  transfers between devices with their start and end apart: 22, of which 8 were waited for; matrix products, arithmetic and copies ran while one was open for 6% of the time, Pallas kernels for 0%

profile of v1, /device:TPU:1, one launch (start us, length us, event | category | flops | bytes accessed | tf_op | source)
XLA Modules:
  0.0 202.7 jit_solution(14543445378059373220)
XLA Ops:
  0.6 0.9 reshape_reshape_reshape.3
  1.6 0.7 copy.183
  2.3 11.4 %all-to-all-start.3 = ((bf16[2,32,512]{2,0,1:T(2,128)(2,1)}), bf16[2,32,512]{2,0,1:T(2,128)(2,1)}, u32[]{:S(2)}, u32[]{:S(2)}) async-start(bf16[2,32,512]{2,0,1:T(2,128)(2,1)} %copy.183), calls=%async_computation.3 | async-start | bytes 131072 | tf_op jit(solution)/shard_map/all_to_all | solution.py:230
  13.8 4.0 %collective-permute-start = (bf16[4,16,64]{2,0,1:T(4,128)(2,1)S(1)}, bf16[4,16,64]{2,0,1:T(4,128)(2,1)S(1)}, u32[]{:S(2)}, u32[]{:S(2)}) collective-permute-start(bf16[4,16,64]{2,0,1:T(4,128)(2,1)S(1)} %copy.173), channel_id=1, source_target_pairs={{0,32},{32,64},{64,96},{96,128},{128,160},{160,192},{192,224},{224... | collective-permute-start | bytes 24584 | tf_op jit(solution)/shard_map/ppermute | solution.py:175
  17.9 1.3 collective-permute-start.1
  19.4 4.2 %all-to-all-done.3 = bf16[2,32,512]{2,0,1:T(2,128)(2,1)} async-done(((bf16[2,32,512]{2,0,1:T(2,128)(2,1)}), bf16[2,32,512]{2,0,1:T(2,128)(2,1)}, u32[]{:S(2)}, u32[]{:S(2)}) %all-to-all-start.3) | async-done | bytes 65568 | tf_op jit(solution)/shard_map/all_to_all | solution.py:230
  23.5 10.2 %all-to-all-start.4 = ((bf16[2,32,512]{2,0,1:T(2,128)(2,1)}), bf16[2,32,512]{2,0,1:T(2,128)(2,1)S(1)}, u32[]{:S(2)}, u32[]{:S(2)}) async-start(bf16[2,32,512]{2,0,1:T(2,128)(2,1)} %all-to-all-done.3), calls=%async_computation.4 | async-start | bytes 131072 | tf_op jit(solution)/shard_map/all_to_all | solution.py:229
  33.8 4.0 %collective-permute-start.2 = (bf16[40,4,64]{2,0,1:T(8,128)(2,1)S(1)}, bf16[40,4,64]{2,0,1:T(8,128)(2,1)S(1)}, u32[]{:S(2)}, u32[]{:S(2)}) collective-permute-start(bf16[40,4,64]{2,0,1:T(8,128)(2,1)S(1)} %get-tuple-element.25), channel_id=1, source_target_pairs={{0,1},{1,2},{2,3},{3,4},{4,5},{5,6},{6,7},{7,8},{8,9},{9,10},{10,1... | collective-permute-start | bytes 61448 | tf_op jit(solution)/shard_map/ppermute | solution.py:175
  37.8 1.9 collective-permute-start.3
  39.7 1.4 all-to-all-done.4
  41.1 0.7 copy.184
  41.8 9.5 %all-to-all-start.5 = ((bf16[32,2,512]{2,1,0:T(2,128)(2,1)}), bf16[32,2,512]{2,1,0:T(2,128)(2,1)S(1)}, u32[]{:S(2)}, u32[]{:S(2)}) async-start(bf16[32,2,512]{2,1,0:T(2,128)(2,1)} %bitcast.10), calls=%async_computation.5 | async-start | bytes 131072 | tf_op jit(solution)/shard_map/all_to_all | solution.py:236
  51.5 0.6 copy-done.3
  52.4 8.7 %all-to-all-done.5 = bf16[32,2,512]{2,1,0:T(2,128)(2,1)S(1)} async-done(((bf16[32,2,512]{2,1,0:T(2,128)(2,1)}), bf16[32,2,512]{2,1,0:T(2,128)(2,1)S(1)}, u32[]{:S(2)}, u32[]{:S(2)}) %all-to-all-start.5) | async-done | bytes 65568 | tf_op jit(solution)/shard_map/all_to_all | solution.py:236
  61.5 2.6 %collective-permute-start.8 = (bf16[4,16,64]{2,1,0:T(8,128)(2,1)S(1)}, bf16[4,16,64]{2,1,0:T(8,128)(2,1)S(1)}, u32[]{:S(2)}, u32[]{:S(2)}) collective-permute-start(bf16[4,16,64]{2,1,0:T(8,128)(2,1)S(1)} %get-tuple-element.29), channel_id=1, source_target_pairs={{0,32},{32,64},{64,96},{96,128},{128,160},{160,192},{192,224},{224... | collective-permute-start | bytes 24584 | tf_op jit(solution)/shard_map/ppermute | solution.py:175
  64.2 1.3 collective-permute-start.9
  65.5 1.0 fusion
  66.5 2.2 %collective-permute-done.9 = bf16[4,16,64]{2,1,0:T(8,128)(2,1)S(1)} collective-permute-done((bf16[4,16,64]{2,1,0:T(8,128)(2,1)S(1)}, bf16[4,16,64]{2,1,0:T(8,128)(2,1)S(1)}, u32[]{:S(2)}, u32[]{:S(2)}) %collective-permute-start.9) | collective-permute-done | bytes 8224 | tf_op jit(solution)/shard_map/ppermute | solution.py:177
  68.7 4.5 %collective-permute-start.10 = (bf16[40,4,64]{2,1,0:T(4,128)(2,1)S(1)}, bf16[40,4,64]{2,1,0:T(4,128)(2,1)S(1)}, u32[]{:S(2)}, u32[]{:S(2)}) collective-permute-start(bf16[40,4,64]{2,1,0:T(4,128)(2,1)S(1)} %get-tuple-element.21), channel_id=1, source_target_pairs={{0,1},{1,2},{2,3},{3,4},{4,5},{5,6},{6,7},{7,8},{8,9},{9,10},{10,1... | collective-permute-start | bytes 61448 | tf_op jit(solution)/shard_map/ppermute | solution.py:175
  73.2 1.9 collective-permute-start.11
  75.4 4.7 %collective-permute-done.11 = bf16[40,4,64]{2,1,0:T(4,128)(2,1)S(1)} collective-permute-done((bf16[40,4,64]{2,1,0:T(4,128)(2,1)S(1)}, bf16[40,4,64]{2,1,0:T(4,128)(2,1)S(1)}, u32[]{:S(2)}, u32[]{:S(2)}) %collective-permute-start.11) | collective-permute-done | bytes 20512 | tf_op jit(solution)/shard_map/ppermute | solution.py:177
  80.2 2.1 %fusion.3 = f32[1,32,16,64]{3,0,2,1:T(1,128)S(1)} fusion(bf16[3,3,64,64]{3,2,1,0:T(8,128)(2,1)S(1)} %copy-done, bf16[1,40,24,64]{3,2,1,0:T(8,128)(2,1)S(1)} %maximum_bitcast_fusion.2), kind=kOutput, calls=%fused_computation.22 | convolution fusion | flops 37748736 | bytes 327680 | tf_op jit(solution)/shard_map/conv_general_dilated | solution.py:189
  82.3 0.6 copy-done.4
  84.9 2.6 %collective-permute-start.4 = (bf16[4,16,64]{2,1,0:T(8,128)(2,1)S(1)}, bf16[4,16,64]{2,1,0:T(8,128)(2,1)S(1)}, u32[]{:S(2)}, u32[]{:S(2)}) collective-permute-start(bf16[4,16,64]{2,1,0:T(8,128)(2,1)S(1)} %get-tuple-element.31), channel_id=1, source_target_pairs={{0,32},{32,64},{64,96},{96,128},{128,160},{160,192},{192,224},{224... | collective-permute-start | bytes 24584 | tf_op jit(solution)/shard_map/ppermute | solution.py:175
  87.5 1.3 collective-permute-start.5
  88.8 4.4 %collective-permute-start.12 = (bf16[4,16,64]{2,1,0:T(8,128)(2,1)S(1)}, bf16[4,16,64]{2,1,0:T(8,128)(2,1)S(1)}, u32[]{:S(2)}, u32[]{:S(2)}) collective-permute-start(bf16[4,16,64]{2,1,0:T(8,128)(2,1)S(1)} %get-tuple-element.27), channel_id=1, source_target_pairs={{0,32},{32,64},{64,96},{96,128},{128,160},{160,192},{192,224},{224... | collective-permute-start | bytes 24584 | tf_op jit(solution)/shard_map/ppermute | solution.py:175
  93.2 1.3 collective-permute-start.13
  95.1 2.5 %collective-permute-start.6 = (bf16[40,4,64]{2,1,0:T(4,128)(2,1)S(1)}, bf16[40,4,64]{2,1,0:T(4,128)(2,1)S(1)}, u32[]{:S(2)}, u32[]{:S(2)}) collective-permute-start(bf16[40,4,64]{2,1,0:T(4,128)(2,1)S(1)} %get-tuple-element.23), channel_id=1, source_target_pairs={{0,1},{1,2},{2,3},{3,4},{4,5},{5,6},{6,7},{7,8},{8,9},{9,10},{10,1... | collective-permute-start | bytes 61448 | tf_op jit(solution)/shard_map/ppermute | solution.py:175
  97.6 1.9 collective-permute-start.7
  99.6 5.1 %collective-permute-start.14 = (bf16[40,4,64]{2,1,0:T(4,128)(2,1)S(1)}, bf16[40,4,64]{2,1,0:T(4,128)(2,1)S(1)}, u32[]{:S(2)}, u32[]{:S(2)}) collective-permute-start(bf16[40,4,64]{2,1,0:T(4,128)(2,1)S(1)} %get-tuple-element.19), channel_id=1, source_target_pairs={{0,1},{1,2},{2,3},{3,4},{4,5},{5,6},{6,7},{7,8},{8,9},{9,10},{10,1... | collective-permute-start | bytes 61448 | tf_op jit(solution)/shard_map/ppermute | solution.py:175
  104.8 1.9 collective-permute-start.15
  108.0 0.5 broadcast.51
  108.5 2.2 %fusion.55 = (f32[32,16,64]{2,1,0:T(8,128)S(1)}, f32[1,32,16,64]{3,0,2,1:T(1,128)S(1)}) fusion(f32[]{:T(128)} %broadcast.51, bf16[3,3,64,64]{3,2,1,0:T(8,128)(2,1)S(1)} %copy-done, bf16[1,40,24,64]{3,2,1,0:T(8,128)(2,1)S(1)} %maximum_bitcast_fusion.1), kind=kOutput, calls=%fused_computation.120 | convolution fusion | flops 37748736 | bytes 458756 | tf_op jit(solution)/shard_map/conv_general_dilated | solution.py:189
  111.1 0.7 copy.179
  111.8 11.5 %all-to-all-start = ((bf16[2,32,512]{2,0,1:T(2,128)(2,1)}), bf16[2,32,512]{2,0,1:T(2,128)(2,1)}, u32[]{:S(2)}, u32[]{:S(2)}) async-start(bf16[2,32,512]{2,0,1:T(2,128)(2,1)} %copy.179), calls=%async_computation | async-start | bytes 131072 | tf_op jit(solution)/shard_map/all_to_all | solution.py:230
  123.4 2.7 %convolution_reduce_fusion = f32[32,16,64]{2,1,0:T(8,128)S(1)} fusion(bf16[3,3,64,64]{3,2,1,0:T(8,128)(2,1)S(1)} %copy-done.5, bf16[1,40,24,64]{3,2,1,0:T(8,128)(2,1)S(1)} %maximum_bitcast_fusion.3), kind=kOutput, calls=%fused_computation | convolution fusion | flops 37748736 | bytes 327680 | tf_op jit(solution)/shard_map/conv_general_dilated | solution.py:189
  126.3 6.8 %all-to-all-done = bf16[2,32,512]{2,0,1:T(2,128)(2,1)} async-done(((bf16[2,32,512]{2,0,1:T(2,128)(2,1)}), bf16[2,32,512]{2,0,1:T(2,128)(2,1)}, u32[]{:S(2)}, u32[]{:S(2)}) %all-to-all-start) | async-done | bytes 65568 | tf_op jit(solution)/shard_map/all_to_all | solution.py:230
  133.1 10.0 %all-to-all-start.1 = ((bf16[2,32,512]{2,0,1:T(2,128)(2,1)}), bf16[2,32,512]{2,0,1:T(2,128)(2,1)S(1)}, u32[]{:S(2)}, u32[]{:S(2)}) async-start(bf16[2,32,512]{2,0,1:T(2,128)(2,1)} %all-to-all-done), calls=%async_computation.1 | async-start | bytes 131072 | tf_op jit(solution)/shard_map/all_to_all | solution.py:229
  143.4 7.1 %all-to-all-done.1 = bf16[2,32,512]{2,0,1:T(2,128)(2,1)S(1)} async-done(((bf16[2,32,512]{2,0,1:T(2,128)(2,1)}), bf16[2,32,512]{2,0,1:T(2,128)(2,1)S(1)}, u32[]{:S(2)}, u32[]{:S(2)}) %all-to-all-start.1) | async-done | bytes 65568 | tf_op jit(solution)/shard_map/all_to_all | solution.py:229
  150.5 0.7 copy.180
  151.2 5.3 %all-to-all-start.2 = ((bf16[32,2,512]{2,1,0:T(2,128)(2,1)}), bf16[32,2,512]{2,1,0:T(2,128)(2,1)S(1)}, u32[]{:S(2)}, u32[]{:S(2)}) async-start(bf16[32,2,512]{2,1,0:T(2,128)(2,1)} %bitcast.5), calls=%async_computation.2 | async-start | bytes 131072 | tf_op jit(solution)/shard_map/all_to_all | solution.py:236
  156.8 9.6 %all-to-all-done.2 = bf16[32,2,512]{2,1,0:T(2,128)(2,1)S(1)} async-done(((bf16[32,2,512]{2,1,0:T(2,128)(2,1)}), bf16[32,2,512]{2,1,0:T(2,128)(2,1)S(1)}, u32[]{:S(2)}, u32[]{:S(2)}) %all-to-all-start.2) | async-done | bytes 65568 | tf_op jit(solution)/shard_map/all_to_all | solution.py:236
  166.9 0.7 convert_reduce_fusion.1
  167.8 0.9 maximum_multiply_fusion.parts
  168.6 30.9 %shard_map.109 = f32[8,10,8,128]{3,2,1,0:T(8,128)} custom-call(f32[8,80,128]{2,1,0:T(8,128)} %maximum_multiply_fusion.parts), custom_call_target="tpu_custom_call" | custom-call | tf_op jit(solution)/shard_map/pallas_call | solution.py:144
  199.5 1.0 slice.201
  200.5 1.3 slice_bitcast_fusion
  201.8 0.9 fusion.50
  (94 shorter events, 7.1 us)
Async XLA Ops:
  0.6 79.5 %copy-start = (bf16[3,3,64,64]{3,2,1,0:T(8,128)(2,1)S(1)}, bf16[3,3,64,64]{3,2,1,0:T(8,128)(2,1)}, u32[]{:S(2)}) copy-start(bf16[3,3,64,64]{3,2,1,0:T(8,128)(2,1)} %param.9) | copy-start | bytes 221188
  2.3 11.4 %copy-start.1 = (bf16[32,1024]{1,0:T(8,128)(2,1)S(1)}, bf16[32,1024]{1,0:T(8,128)(2,1)}, u32[]{:S(2)}) copy-start(bf16[32,1024]{1,0:T(8,128)(2,1)} %param.6) | copy-start | bytes 196612
  2.3 21.3 %all-to-all-start.3 = ((bf16[2,32,512]{2,0,1:T(2,128)(2,1)}), bf16[2,32,512]{2,0,1:T(2,128)(2,1)}, u32[]{:S(2)}, u32[]{:S(2)}) async-start(bf16[2,32,512]{2,0,1:T(2,128)(2,1)} %copy.183), calls=%async_computation.3 | async-start | bytes 131072 | tf_op jit(solution)/shard_map/all_to_all | solution.py:230
  13.8 19.9 %collective-permute-start = (bf16[4,16,64]{2,0,1:T(4,128)(2,1)S(1)}, bf16[4,16,64]{2,0,1:T(4,128)(2,1)S(1)}, u32[]{:S(2)}, u32[]{:S(2)}) collective-permute-start(bf16[4,16,64]{2,0,1:T(4,128)(2,1)S(1)} %copy.173), channel_id=1, source_target_pairs={{0,32},{32,64},{64,96},{96,128},{128,160},{160,192},{192,224},{224... | collective-permute-start | bytes 24584 | tf_op jit(solution)/shard_map/ppermute | solution.py:175
  17.9 15.8 %collective-permute-start.1 = (bf16[4,16,64]{2,0,1:T(4,128)(2,1)S(1)}, bf16[4,16,64]{2,0,1:T(4,128)(2,1)S(1)}, u32[]{:S(2)}, u32[]{:S(2)}) collective-permute-start(bf16[4,16,64]{2,0,1:T(4,128)(2,1)S(1)} %copy.174), channel_id=1, source_target_pairs={{32,0},{64,32},{96,64},{128,96},{160,128},{192,160},{224,192},{256... | collective-permute-start | bytes 24584 | tf_op jit(solution)/shard_map/ppermute | solution.py:177
  23.5 17.5 %all-to-all-start.4 = ((bf16[2,32,512]{2,0,1:T(2,128)(2,1)}), bf16[2,32,512]{2,0,1:T(2,128)(2,1)S(1)}, u32[]{:S(2)}, u32[]{:S(2)}) async-start(bf16[2,32,512]{2,0,1:T(2,128)(2,1)} %all-to-all-done.3), calls=%async_computation.4 | async-start | bytes 131072 | tf_op jit(solution)/shard_map/all_to_all | solution.py:229
  33.8 18.5 %collective-permute-start.2 = (bf16[40,4,64]{2,0,1:T(8,128)(2,1)S(1)}, bf16[40,4,64]{2,0,1:T(8,128)(2,1)S(1)}, u32[]{:S(2)}, u32[]{:S(2)}) collective-permute-start(bf16[40,4,64]{2,0,1:T(8,128)(2,1)S(1)} %get-tuple-element.25), channel_id=1, source_target_pairs={{0,1},{1,2},{2,3},{3,4},{4,5},{5,6},{6,7},{7,8},{8,9},{9,10},{10,1... | collective-permute-start | bytes 61448 | tf_op jit(solution)/shard_map/ppermute | solution.py:175
  37.8 14.6 %collective-permute-start.3 = (bf16[40,4,64]{2,0,1:T(8,128)(2,1)S(1)}, bf16[40,4,64]{2,0,1:T(8,128)(2,1)S(1)}, u32[]{:S(2)}, u32[]{:S(2)}) collective-permute-start(bf16[40,4,64]{2,0,1:T(8,128)(2,1)S(1)} %get-tuple-element.26), channel_id=1, source_target_pairs={{1,0},{2,1},{3,2},{4,3},{5,4},{6,5},{7,6},{8,7},{9,8},{10,9},{11,1... | collective-permute-start | bytes 61448 | tf_op jit(solution)/shard_map/ppermute | solution.py:177
  41.8 9.6 %copy-start.2 = (bf16[32,1024]{1,0:T(8,128)(2,1)S(1)}, bf16[32,1024]{1,0:T(8,128)(2,1)}, u32[]{:S(2)}) copy-start(bf16[32,1024]{1,0:T(8,128)(2,1)} %param.11) | copy-start | bytes 196612
  41.8 19.4 %all-to-all-start.5 = ((bf16[32,2,512]{2,1,0:T(2,128)(2,1)}), bf16[32,2,512]{2,1,0:T(2,128)(2,1)S(1)}, u32[]{:S(2)}, u32[]{:S(2)}) async-start(bf16[32,2,512]{2,1,0:T(2,128)(2,1)} %bitcast.10), calls=%async_computation.5 | async-start | bytes 131072 | tf_op jit(solution)/shard_map/all_to_all | solution.py:236
  51.5 0.7 copy-start.3
  61.4 4.0 %copy-start.5 = (bf16[3,3,64,64]{3,2,1,0:T(8,128)(2,1)S(1)}, bf16[3,3,64,64]{3,2,1,0:T(8,128)(2,1)}, u32[]{:S(2)}) copy-start(bf16[3,3,64,64]{3,2,1,0:T(8,128)(2,1)} %param.7) | copy-start | bytes 221188
  61.5 4.9 %collective-permute-start.8 = (bf16[4,16,64]{2,1,0:T(8,128)(2,1)S(1)}, bf16[4,16,64]{2,1,0:T(8,128)(2,1)S(1)}, u32[]{:S(2)}, u32[]{:S(2)}) collective-permute-start(bf16[4,16,64]{2,1,0:T(8,128)(2,1)S(1)} %get-tuple-element.29), channel_id=1, source_target_pairs={{0,32},{32,64},{64,96},{96,128},{128,160},{160,192},{192,224},{224... | collective-permute-start | bytes 24584 | tf_op jit(solution)/shard_map/ppermute | solution.py:175
  64.2 4.5 %collective-permute-start.9 = (bf16[4,16,64]{2,1,0:T(8,128)(2,1)S(1)}, bf16[4,16,64]{2,1,0:T(8,128)(2,1)S(1)}, u32[]{:S(2)}, u32[]{:S(2)}) collective-permute-start(bf16[4,16,64]{2,1,0:T(8,128)(2,1)S(1)} %get-tuple-element.30), channel_id=1, source_target_pairs={{32,0},{64,32},{96,64},{128,96},{160,128},{192,160},{224,192},{256... | collective-permute-start | bytes 24584 | tf_op jit(solution)/shard_map/ppermute | solution.py:177
  68.7 6.7 %collective-permute-start.10 = (bf16[40,4,64]{2,1,0:T(4,128)(2,1)S(1)}, bf16[40,4,64]{2,1,0:T(4,128)(2,1)S(1)}, u32[]{:S(2)}, u32[]{:S(2)}) collective-permute-start(bf16[40,4,64]{2,1,0:T(4,128)(2,1)S(1)} %get-tuple-element.21), channel_id=1, source_target_pairs={{0,1},{1,2},{2,3},{3,4},{4,5},{5,6},{6,7},{7,8},{8,9},{9,10},{10,1... | collective-permute-start | bytes 61448 | tf_op jit(solution)/shard_map/ppermute | solution.py:175
  73.2 6.8 %collective-permute-start.11 = (bf16[40,4,64]{2,1,0:T(4,128)(2,1)S(1)}, bf16[40,4,64]{2,1,0:T(4,128)(2,1)S(1)}, u32[]{:S(2)}, u32[]{:S(2)}) collective-permute-start(bf16[40,4,64]{2,1,0:T(4,128)(2,1)S(1)} %get-tuple-element.22), channel_id=1, source_target_pairs={{1,0},{2,1},{3,2},{4,3},{5,4},{6,5},{7,6},{8,7},{9,8},{10,9},{11,1... | collective-permute-start | bytes 61448 | tf_op jit(solution)/shard_map/ppermute | solution.py:177
  82.3 0.7 copy-start.4
  84.9 10.2 %collective-permute-start.4 = (bf16[4,16,64]{2,1,0:T(8,128)(2,1)S(1)}, bf16[4,16,64]{2,1,0:T(8,128)(2,1)S(1)}, u32[]{:S(2)}, u32[]{:S(2)}) collective-permute-start(bf16[4,16,64]{2,1,0:T(8,128)(2,1)S(1)} %get-tuple-element.31), channel_id=1, source_target_pairs={{0,32},{32,64},{64,96},{96,128},{128,160},{160,192},{192,224},{224... | collective-permute-start | bytes 24584 | tf_op jit(solution)/shard_map/ppermute | solution.py:175
  87.5 7.5 %collective-permute-start.5 = (bf16[4,16,64]{2,1,0:T(8,128)(2,1)S(1)}, bf16[4,16,64]{2,1,0:T(8,128)(2,1)S(1)}, u32[]{:S(2)}, u32[]{:S(2)}) collective-permute-start(bf16[4,16,64]{2,1,0:T(8,128)(2,1)S(1)} %get-tuple-element.32), channel_id=1, source_target_pairs={{32,0},{64,32},{96,64},{128,96},{160,128},{192,160},{224,192},{256... | collective-permute-start | bytes 24584 | tf_op jit(solution)/shard_map/ppermute | solution.py:177
  88.8 10.7 %collective-permute-start.12 = (bf16[4,16,64]{2,1,0:T(8,128)(2,1)S(1)}, bf16[4,16,64]{2,1,0:T(8,128)(2,1)S(1)}, u32[]{:S(2)}, u32[]{:S(2)}) collective-permute-start(bf16[4,16,64]{2,1,0:T(8,128)(2,1)S(1)} %get-tuple-element.27), channel_id=1, source_target_pairs={{0,32},{32,64},{64,96},{96,128},{128,160},{160,192},{192,224},{224... | collective-permute-start | bytes 24584 | tf_op jit(solution)/shard_map/ppermute | solution.py:175
  93.2 6.3 %collective-permute-start.13 = (bf16[4,16,64]{2,1,0:T(8,128)(2,1)S(1)}, bf16[4,16,64]{2,1,0:T(8,128)(2,1)S(1)}, u32[]{:S(2)}, u32[]{:S(2)}) collective-permute-start(bf16[4,16,64]{2,1,0:T(8,128)(2,1)S(1)} %get-tuple-element.28), channel_id=1, source_target_pairs={{32,0},{64,32},{96,64},{128,96},{160,128},{192,160},{224,192},{256... | collective-permute-start | bytes 24584 | tf_op jit(solution)/shard_map/ppermute | solution.py:177
  95.1 12.0 %collective-permute-start.6 = (bf16[40,4,64]{2,1,0:T(4,128)(2,1)S(1)}, bf16[40,4,64]{2,1,0:T(4,128)(2,1)S(1)}, u32[]{:S(2)}, u32[]{:S(2)}) collective-permute-start(bf16[40,4,64]{2,1,0:T(4,128)(2,1)S(1)} %get-tuple-element.23), channel_id=1, source_target_pairs={{0,1},{1,2},{2,3},{3,4},{4,5},{5,6},{6,7},{7,8},{8,9},{9,10},{10,1... | collective-permute-start | bytes 61448 | tf_op jit(solution)/shard_map/ppermute | solution.py:175
  97.6 9.5 %collective-permute-start.7 = (bf16[40,4,64]{2,1,0:T(4,128)(2,1)S(1)}, bf16[40,4,64]{2,1,0:T(4,128)(2,1)S(1)}, u32[]{:S(2)}, u32[]{:S(2)}) collective-permute-start(bf16[40,4,64]{2,1,0:T(4,128)(2,1)S(1)} %get-tuple-element.24), channel_id=1, source_target_pairs={{1,0},{2,1},{3,2},{4,3},{5,4},{6,5},{7,6},{8,7},{9,8},{10,9},{11,1... | collective-permute-start | bytes 61448 | tf_op jit(solution)/shard_map/ppermute | solution.py:177
  99.6 23.6 %collective-permute-start.14 = (bf16[40,4,64]{2,1,0:T(4,128)(2,1)S(1)}, bf16[40,4,64]{2,1,0:T(4,128)(2,1)S(1)}, u32[]{:S(2)}, u32[]{:S(2)}) collective-permute-start(bf16[40,4,64]{2,1,0:T(4,128)(2,1)S(1)} %get-tuple-element.19), channel_id=1, source_target_pairs={{0,1},{1,2},{2,3},{3,4},{4,5},{5,6},{6,7},{7,8},{8,9},{9,10},{10,1... | collective-permute-start | bytes 61448 | tf_op jit(solution)/shard_map/ppermute | solution.py:175
  104.8 18.5 %collective-permute-start.15 = (bf16[40,4,64]{2,1,0:T(4,128)(2,1)S(1)}, bf16[40,4,64]{2,1,0:T(4,128)(2,1)S(1)}, u32[]{:S(2)}, u32[]{:S(2)}) collective-permute-start(bf16[40,4,64]{2,1,0:T(4,128)(2,1)S(1)} %get-tuple-element.20), channel_id=1, source_target_pairs={{1,0},{2,1},{3,2},{4,3},{5,4},{6,5},{7,6},{8,7},{9,8},{10,9},{11,1... | collective-permute-start | bytes 61448 | tf_op jit(solution)/shard_map/ppermute | solution.py:177
  111.8 21.3 %all-to-all-start = ((bf16[2,32,512]{2,0,1:T(2,128)(2,1)}), bf16[2,32,512]{2,0,1:T(2,128)(2,1)}, u32[]{:S(2)}, u32[]{:S(2)}) async-start(bf16[2,32,512]{2,0,1:T(2,128)(2,1)} %copy.179), calls=%async_computation | async-start | bytes 131072 | tf_op jit(solution)/shard_map/all_to_all | solution.py:230
  133.1 17.4 %all-to-all-start.1 = ((bf16[2,32,512]{2,0,1:T(2,128)(2,1)}), bf16[2,32,512]{2,0,1:T(2,128)(2,1)S(1)}, u32[]{:S(2)}, u32[]{:S(2)}) async-start(bf16[2,32,512]{2,0,1:T(2,128)(2,1)} %all-to-all-done), calls=%async_computation.1 | async-start | bytes 131072 | tf_op jit(solution)/shard_map/all_to_all | solution.py:229
  151.2 15.3 %all-to-all-start.2 = ((bf16[32,2,512]{2,1,0:T(2,128)(2,1)}), bf16[32,2,512]{2,1,0:T(2,128)(2,1)S(1)}, u32[]{:S(2)}, u32[]{:S(2)}) async-start(bf16[32,2,512]{2,1,0:T(2,128)(2,1)} %bitcast.5), calls=%async_computation.2 | async-start | bytes 131072 | tf_op jit(solution)/shard_map/all_to_all | solution.py:236

commit v2 on v0

v2 whole, which is shorter than its diff:
```python
import jax
import jax.numpy as jnp
from jax import lax
from jax.experimental import pallas as pl
from jax.experimental.pallas import tpu as pltpu
from jax.sharding import PartitionSpec as P

MESH = pl.DeviceIdType.MESH
F32 = jnp.float32
BF16 = jnp.bfloat16
CH = 64
ROWS = 32
WIDTH = 1024
QUAD = 256
INV_BINS = 1.0 / 512
PLANE = 32
DEPTH = 8
LINES = 10
SLOPE = 0.7978845608
CUBIC = 0.044715
AROUND = tuple((a, b) for a in (-1, 0, 1) for b in (-1, 0, 1) if a or b)
ENDS = {-1: (pl.ds(1, 1), pl.ds(5, 1)), 0: (pl.ds(1, 4), pl.ds(1, 4)), 1: (pl.ds(4, 1), pl.ds(0, 1))}
SIDES = {-1: (pl.ds(1, 1), pl.ds(3, 1)), 0: (pl.ds(1, 2), pl.ds(1, 2)), 1: (pl.ds(2, 1), pl.ds(0, 1))}


def plane_id(row, col, peer):
    return (lax.rem(peer, 2) * 8 + lax.rem(row, 8), (peer // 2) * 2 + lax.rem(col, 2))


def depth_id(row, col, peer):
    return ((row // 8) * 8 + peer, col)


def block_of(taps, transpose):
    zero = jnp.zeros((CH, CH), F32)
    value = taps.astype(F32)
    if transpose:
        value = value.T
    left = jnp.concatenate([value, zero], axis=1).astype(BF16)
    right = jnp.concatenate([zero, value], axis=1).astype(BF16)
    return left, right


def fill(matrix, taps_ref, flip):
    matrix[...] = jnp.zeros(matrix.shape, BF16)
    for a in range(3):
        for b in range(3):
            if flip:
                left, right = block_of(taps_ref[2 - a, 2 - b], True)
            else:
                left, right = block_of(taps_ref[a, b], False)
            for k in range(4):
                rows = pl.ds(b * QUAD + k * CH, CH)
                cols = pl.ds(a * QUAD + (k // 2) * 128, 128)
                matrix[rows, cols] = right if k % 2 else left


def pack(own, padded):
    for q in range(4):
        for g in range(2):
            rows = own[8 * q : 8 * q + 8]
            pair = [rows[:, QUAD * (2 * g + s) : QUAD * (2 * g + s + 1)] for s in range(2)]
            padded[q + 1, g + 1] = jnp.concatenate(pair, axis=0).astype(BF16)


def unpack(padded):
    values = padded[...].astype(F32)
    return [
        jnp.concatenate([values[q, g // 2, 8 * (g % 2) : 8 * (g % 2) + 8] for q in range(6)], axis=0).astype(BF16)
        for g in range(8)
    ]


def clear_edges(padded, row, col):
    @pl.when(row == 0)
    def _():
        padded[0] = jnp.zeros((4, 16, QUAD), BF16)

    @pl.when(row == 15)
    def _():
        padded[5] = jnp.zeros((4, 16, QUAD), BF16)

    @pl.when(col == 0)
    def _():
        padded[:, 0] = jnp.zeros((6, 16, QUAD), BF16)

    @pl.when(col == 31)
    def _():
        padded[:, 3] = jnp.zeros((6, 16, QUAD), BF16)


def conv(groups, matrix, rows):
    count = len(groups) - 2
    left = jnp.concatenate([jnp.stack(groups[b : b + count]) for b in range(3)], axis=-1)
    full = jnp.dot(left.reshape(count * 48, 3 * QUAD), matrix[...], preferred_element_type=F32)
    full = full.reshape(count, 48, 3 * QUAD)
    return (
        full[:, 0:rows, 0:QUAD]
        + full[:, 4 : 4 + rows, QUAD : 2 * QUAD]
        + full[:, 8 : 8 + rows, 2 * QUAD :]
    )


def taps_of(groups, grads):
    count, rows = grads.shape[:2]
    shifted = []
    for a in range(3):
        parts = [grads]
        if a:
            parts.insert(0, jnp.zeros((count, 4 * a, QUAD), F32))
        if 48 - rows - 4 * a:
            parts.append(jnp.zeros((count, 48 - rows - 4 * a, QUAD), F32))
        shifted.append(jnp.concatenate(parts, axis=1) if len(parts) > 1 else grads)
    right = jnp.concatenate(shifted, axis=-1).astype(BF16).reshape(count * 48, 3 * QUAD)
    out = []
    for b in range(3):
        left = jnp.stack(groups[b : b + count]).reshape(count * 48, QUAD)
        out.append(lax.dot_general(left, right, (((0,), (0,)), ((), ())), preferred_element_type=F32))
    return out


def halves(full, a):
    one = full[:, a * QUAD : a * QUAD + 128]
    two = full[:, a * QUAD + 128 : (a + 1) * QUAD]
    return one[0:64] + two[128:192], one[64:128] + two[192:256]


def turned(block, spare, base):
    lane = lax.broadcasted_iota(jnp.int32, (8, 128), 1)
    for p in range(8):
        spare[pl.ds(base + 16 * p, 16), :] = block[:, 128 * p : 128 * p + 128]
    for p in range(8):
        even = spare[pl.ds(base + 16 * p, 8, stride=2), :]
        odd = spare[pl.ds(base + 16 * p + 1, 8, stride=2), :]
        spare[pl.ds(base + 128 + 16 * p, 8), :] = jnp.where(lane < 64, even, pltpu.roll(odd, 64, 1))
        spare[pl.ds(base + 128 + 16 * p + 8, 8), :] = jnp.where(lane < 64, pltpu.roll(even, 64, 1), odd)
    return jnp.concatenate([spare[pl.ds(base + 128 + q, 16, stride=8), :] for q in range(8)], axis=1)


def grouped(tile):
    return jnp.stack([tile[:, QUAD * g : QUAD * (g + 1)] for g in range(4)])


def kernel(
    act_hbm, cot_hbm, one_hbm, two_hbm, bias_one, bias_two,
    sym_out, grad_out, full,
    act, cot, one, two, mat_one, mat_two, back_one, back_two,
    source_pad, sym_pad, mirror, summed, mirror_sum, spare,
    parts, core_in, plane_in, depth_in, piece,
    load_sem, m_send, m_recv, s_send, s_recv, x_send, x_recv, g_send, g_recv, ar_send, ar_recv,
):
    row, col = lax.axis_index("row"), lax.axis_index("col")
    core = lax.rem(col, 2)
    plane = (col // 2) * 2 + row // 8
    depth = lax.rem(row, 8)
    sibling = (row, col + 1 - 2 * core)
    around = [(lax.rem(row + a + 16, 16), lax.rem(col + b + 32, 32)) for a, b in AROUND]
    opposite = [(col // 2, 2 * row + h) for h in range(2)]
    diagonal = col // 2 == row
    is_self = [diagonal & (core == h) for h in range(2)]

    barrier = pltpu.get_barrier_semaphore()
    for h in range(2):
        @pl.when(jnp.logical_not(is_self[h]))
        def _():
            pl.semaphore_signal(barrier, inc=1, device_id=opposite[h], device_id_type=MESH)
    for device in around + [sibling]:
        pl.semaphore_signal(barrier, inc=1, device_id=device, device_id_type=MESH)

    @pl.loop(1, PLANE)
    def _(step):
        pl.semaphore_signal(barrier, inc=1, device_id=plane_id(row, col, lax.rem(plane + step, PLANE)), device_id_type=MESH)

    @pl.loop(1, DEPTH)
    def _(step):
        pl.semaphore_signal(barrier, inc=1, device_id=depth_id(row, col, lax.rem(depth + step, DEPTH)), device_id_type=MESH)

    loads = [
        pltpu.make_async_copy(src, dst, load_sem.at[k])
        for k, (src, dst) in enumerate(((act_hbm, act), (one_hbm, one), (two_hbm, two), (cot_hbm, cot)))
    ]
    for copy in loads:
        copy.start()
    loads[0].wait()
    source = act[...].astype(F32)
    pack(source, source_pad)

    def swap_start(src, dst, send, recv):
        for h in range(2):
            @pl.when(jnp.logical_not(is_self[h]))
            def _():
                pltpu.make_async_remote_copy(
                    src_ref=src.at[pl.ds(16 * h, 16)], dst_ref=dst.at[core], send_sem=send.at[h], recv_sem=recv.at[core],
                    device_id=opposite[h], device_id_type=MESH,
                ).start()

            @pl.when(is_self[h])
            def _():
                pltpu.make_async_copy(src.at[pl.ds(16 * h, 16)], dst.at[core], recv.at[core]).start()

    def swap_sent(src, dst, send):
        for h in range(2):
            @pl.when(jnp.logical_not(is_self[h]))
            def _():
                pltpu.make_async_copy(src.at[pl.ds(16 * h, 16)], dst.at[h], send.at[h]).wait()

    def halo_start(padded, send, recv):
        copies = []
        for k, (a, b) in enumerate(AROUND):
            copies.append(
                pltpu.make_async_remote_copy(
                    src_ref=padded.at[ENDS[a][0], SIDES[b][0]], dst_ref=padded.at[ENDS[a][1], SIDES[b][1]],
                    send_sem=send.at[k], recv_sem=recv.at[k], device_id=around[k], device_id_type=MESH,
                )
            )
            copies[-1].start()
        return copies

    pl.semaphore_wait(barrier, 2 + 8 + 1 + PLANE - 1 + DEPTH - 1 - diagonal.astype(jnp.int32))
    swap_start(cot_hbm, mirror, m_send, m_recv)
    source_halo = halo_start(source_pad, s_send, s_recv)

    loads[1].wait()
    loads[2].wait()
    fill(mat_one, one, False)
    fill(mat_two, two, False)
    fill(back_two, two, True)
    fill(back_one, one, True)
    parts[8:CH, 9, :] = jnp.zeros((CH - 8, 128), F32)

    line = lax.broadcasted_iota(jnp.int32, (40, QUAD), 0)
    inside = ((line >= 4) | (row > 0)) & ((line < 36) | (row < 15))
    first = inside & (col > 0)
    last = inside & (col < 31)

    def masked(values):
        return jnp.stack([jnp.where((first, inside, inside, inside, inside, last)[g], values[g], 0.0) for g in range(6)])

    for copy in source_halo:
        copy.wait_recv()
    clear_edges(source_pad, row, col)
    source_groups = unpack(source_pad)
    wide_one = jnp.concatenate([bias_one[...]] * 4, axis=1)
    wide_two = jnp.concatenate([bias_two[...]] * 4, axis=1)
    preact = conv(source_groups, mat_one, 40) + wide_one
    bent = jnp.tanh(SLOPE * (preact + CUBIC * preact * preact * preact))
    hidden = masked(0.5 * preact * (1.0 + bent))
    slope = masked(
        0.5 * (1.0 + bent)
        + 0.5 * preact * (1.0 - bent * bent) * (SLOPE * (1.0 + 3.0 * CUBIC * preact * preact))
    )
    blank = jnp.zeros((6, 8, QUAD), F32)
    hidden = jnp.concatenate([hidden, blank], axis=1).astype(BF16)
    hidden_groups = [hidden[g] for g in range(6)]
    branch = conv(hidden_groups, mat_two, 32) + wide_two
    summed[...] = (source + jnp.concatenate([branch[g] for g in range(4)], axis=1)).astype(BF16)

    loads[3].wait()
    for h in range(2):
        pltpu.make_async_copy(mirror.at[h], mirror.at[h], m_recv.at[h]).wait()
    turned_cot = jnp.concatenate([turned(mirror[h].astype(F32), spare, 256 * h) for h in range(2)], axis=0)
    sym = ((cot[...].astype(F32) + turned_cot) * 0.5).astype(BF16).astype(F32)
    pack(sym, sym_pad)
    sym_halo = halo_start(sym_pad, g_send, g_recv)
    swap_start(summed, mirror_sum, x_send, x_recv)

    sym_own = grouped(sym)
    lower = jnp.zeros((4, 8, QUAD), F32)
    sym_rows = jnp.concatenate([lower, sym_own, lower], axis=1).astype(BF16)
    nothing = jnp.zeros((48, QUAD), BF16)
    sym_groups = [nothing] * 2 + [sym_rows[g] for g in range(4)] + [nothing] * 2
    share = conv(sym_groups, back_two, 40) * slope
    taps_two = taps_of(hidden_groups, sym_own)
    taps_one = taps_of(source_groups, share)
    left = lax.broadcasted_iota(jnp.int32, (CH, 128), 1) < CH
    for a in range(3):
        for b in range(3):
            near_one, far_one = halves(taps_one[b], a)
            near_two, far_two = halves(taps_two[b], a)
            parts[:, 3 * a + b, :] = jnp.where(
                left, near_one + pltpu.roll(far_one, CH, 1), far_two + pltpu.roll(near_two, CH, 1)
            )
    bias = []
    for grads in (share, sym_own):
        total = jnp.sum(grads.reshape(-1, 8, QUAD), axis=0)
        total = total[:, :128] + total[:, 128:]
        bias.append(total + pltpu.roll(total, CH, 1))
    parts[0:8, 9, :] = jnp.where(left[:8], bias[0], bias[1])

    own = pl.ds(PLANE * core, PLANE)
    to_core = pltpu.make_async_remote_copy(
        src_ref=parts.at[pl.ds(PLANE * (1 - core), PLANE)], dst_ref=core_in, send_sem=ar_send.at[0], recv_sem=ar_recv.at[0],
        device_id=sibling, device_id_type=MESH,
    )
    to_core.start()
    to_core.wait_recv()
    core_in[...] = core_in[...] + parts[own]

    @pl.loop(1, PLANE)
    def _(step):
        peer = lax.rem(plane + step, PLANE)
        pltpu.make_async_remote_copy(
            src_ref=core_in.at[peer], dst_ref=plane_in.at[step - 1], send_sem=ar_send.at[1], recv_sem=ar_recv.at[1],
            device_id=plane_id(row, col, peer), device_id_type=MESH,
        ).start()

    for copy in sym_halo:
        copy.wait_recv()
    clear_edges(sym_pad, row, col)
    pre_grad = conv(unpack(sym_pad), back_two, 40) * slope
    pre_grad = jnp.concatenate([pre_grad, blank], axis=1).astype(BF16)
    input_grad = conv([pre_grad[g] for g in range(6)], back_one, 32)
    grad_out[...] = (sym + jnp.concatenate([input_grad[g] for g in range(4)], axis=1)).astype(BF16)

    pltpu.make_async_copy(plane_in, plane_in, ar_recv.at[1]).wait()
    depth_in[depth] = jnp.sum(plane_in[...], axis=0) + core_in[plane]

    @pl.loop(1, DEPTH)
    def _(step):
        peer = lax.rem(depth + step, DEPTH)
        pltpu.make_async_remote_copy(
            src_ref=depth_in.at[depth], dst_ref=depth_in.at[depth], send_sem=ar_send.at[2], recv_sem=ar_recv.at[2],
            device_id=depth_id(row, col, peer), device_id_type=MESH,
        ).start()

    for h in range(2):
        pltpu.make_async_copy(mirror_sum.at[h], mirror_sum.at[h], x_recv.at[h]).wait()
    turned_sum = jnp.concatenate([turned(mirror_sum[h].astype(F32), spare, 256 * h) for h in range(2)], axis=0)
    sym_out[...] = ((summed[...].astype(F32) + turned_sum) * 0.5).astype(BF16)

    pltpu.make_async_copy(depth_in.at[pl.ds(0, DEPTH - 1)], depth_in.at[pl.ds(0, DEPTH - 1)], ar_recv.at[2]).wait()
    here = PLANE * core + plane
    full[here] = jnp.sum(depth_in[...], axis=0) * INV_BINS

    @pl.loop(1, PLANE)
    def _(step):
        pltpu.make_async_remote_copy(
            src_ref=full.at[here], dst_ref=full.at[here], send_sem=ar_send.at[3], recv_sem=ar_recv.at[3],
            device_id=plane_id(row, col, lax.rem(plane + step, PLANE)), device_id_type=MESH,
        ).start()

    pltpu.make_async_copy(plane_in, plane_in, ar_recv.at[3]).wait()
    back_core = pltpu.make_async_remote_copy(
        src_ref=full.at[own], dst_ref=full.at[own], send_sem=ar_send.at[4], recv_sem=ar_recv.at[4],
        device_id=sibling, device_id_type=MESH,
    )
    back_core.start()
    swap_sent(cot_hbm, mirror, m_send)
    swap_sent(summed, mirror_sum, x_send)
    for copy in source_halo + sym_halo + [to_core]:
        copy.wait_send()
    pltpu.make_async_copy(plane_in, plane_in, ar_send.at[1]).wait()
    pltpu.make_async_copy(depth_in.at[pl.ds(0, DEPTH - 1)], depth_in.at[pl.ds(0, DEPTH - 1)], ar_send.at[2]).wait()
    pltpu.make_async_copy(plane_in, plane_in, ar_send.at[3]).wait()
    back_core.wait()


def on_device(activations, conv_one, bias_one, conv_two, bias_two, cotangent):
    vmem, anywhere = pl.BlockSpec(memory_space=pltpu.VMEM), pl.BlockSpec(memory_space=pl.ANY)
    dma = pltpu.SemaphoreType.DMA
    tile = jax.ShapeDtypeStruct((ROWS, WIDTH), BF16)
    symmetric_out, input_grad, full = pl.pallas_call(
        kernel,
        out_shape=(tile, tile, jax.ShapeDtypeStruct((CH, LINES, 128), F32)),
        in_specs=[anywhere] * 4 + [vmem] * 2,
        out_specs=[vmem] * 3,
        scratch_shapes=[
            pltpu.VMEM((ROWS, WIDTH), BF16),
            pltpu.VMEM((ROWS, WIDTH), BF16),
            pltpu.VMEM((3, 3, CH, CH), BF16),
            pltpu.VMEM((3, 3, CH, CH), BF16),
        ]
        + [pltpu.VMEM((3 * QUAD, 3 * QUAD), BF16)] * 4
        + [
            pltpu.VMEM((6, 4, 16, QUAD), BF16),
            pltpu.VMEM((6, 4, 16, QUAD), BF16),
            pltpu.VMEM((2, 16, WIDTH), BF16),
            pltpu.VMEM((ROWS, WIDTH), BF16),
            pltpu.VMEM((2, 16, WIDTH), BF16),
            pltpu.VMEM((512, 128), F32),
            pltpu.VMEM((CH, LINES, 128), F32),
            pltpu.VMEM((PLANE, LINES, 128), F32),
            pltpu.VMEM((PLANE - 1, LINES, 128), F32),
            pltpu.VMEM((DEPTH, LINES, 128), F32),
            pltpu.VMEM((LINES, 128), F32),
            dma((4,)), dma((2,)), dma((2,)), dma((8,)), dma((8,)), dma((2,)), dma((2,)), dma((8,)), dma((8,)), dma((5,)), dma((5,)),
        ],
        compiler_params=pltpu.CompilerParams(collective_id=0, has_side_effects=True, vmem_limit_bytes=48 * 1024 * 1024),
    )(activations, cotangent, conv_one, conv_two, bias_one.reshape(1, CH), bias_two.reshape(1, CH))
    taps = jnp.swapaxes(full[:, :9], 0, 1).reshape(3, 3, CH, 2 * CH)
    biases = jnp.sum(full[:, 9], axis=0)
    return symmetric_out, input_grad, taps[..., :CH], biases[:CH], taps[..., CH:], biases[CH:]


def solution(mesh):
    return jax.shard_map(
        on_device,
        mesh=mesh,
        in_specs=(P("row", "col"), P(), P(), P(), P(), P("row", "col")),
        out_specs=(P("row", "col"), P("row", "col"), P(), P(), P(), P()),
        check_vma=False,
    )
```

time: 441 us -> 71.6 us (0.16)
  waiting for transfers between devices: 201 us -> 0 us
  starting transfers between devices: 100 us -> 0 us
  blocking collectives: 98.1 us -> 0 us
  Pallas kernels: 0 us -> 63.6 us
  between operations: 14.7 us -> 0.68 us
  matrix products: 11.6 us -> 0 us
    psum x1 -> x0, waiting for transfers between devices: 160 us -> none  [on_device(): lax.psum((kernel_grad(padded_in, pre_grad) * inv_bins, jnp.sum(pre_grad,...]
    psum x1 -> x0, blocking collectives: 98.1 us -> none  [on_device(): lax.psum((kernel_grad(padded_in, pre_grad) * inv_bins, jnp.sum(pre_grad,...]
    pallas_call x0 -> x1, Pallas kernels: none -> 63.6 us  [on_device(): pl.pallas_call(kernel, out_shape=(tile, tile, jax.ShapeDtypeStruct((CH, L...]
    all_to_all x6 -> x0, starting transfers between devices: 57.4 us -> none  [the longest x2 22.3 us: mirror_tile(): lax.all_to_all(sectioned, 'col', split_axis=1, concat_axis=1, tiled=True)]
    ppermute x16 -> x0, starting transfers between devices: 42.8 us -> none  [the longest x8 29.8 us: padded_2(): lax.ppermute(tail, axis, [(i, (i + 1) % count) for i in range(ends)])]
    all_to_all x6 -> x0, waiting for transfers between devices: 29.6 us -> none  [the longest x2 13.1 us: mirror_tile(): lax.all_to_all(sectioned, 'col', split_axis=1, concat_axis=1, tiled=True)]
    ppermute x16 -> x0, waiting for transfers between devices: 11.2 us -> none  [the longest x8 11.1 us: padded_2(): lax.ppermute(head, axis, [((i + 1) % count, i) for i in range(ends)])]
    conv_general_dilated x4 -> x0, matrix products: 7.95 us -> none  [dilated(): lax.conv_general_dilated(padded[None], kernel, (1, 1), 'VALID', rhs_dilat...]
  transfers between devices with their start and end apart: 23 -> 0, of which waited for: 9 -> 0; matrix products, arithmetic and copies ran while one was open for 2% -> 0% of each run, Pallas kernels for 0% -> 0%
where the time goes in v2:
time: 71.6 us; the launch traced here: 71.4 us
  Pallas kernels  63.6 us (89%)
  local copies, waits for them, and re-layouts  7.02 us (10%)
    pallas_call x1, Pallas kernels, on_device(): pl.pallas_call(kernel, out_shape=(tile, tile, jax.ShapeDtypeStruct((CH, L...  63.6 us
    unnamed x14, local copies, waits for them, and re-layouts  5.41 us

profile of v2, /device:TPU:1, one launch (start us, length us, event | category | flops | bytes accessed | tf_op | source)
XLA Modules:
  0.0 71.4 jit_solution(5939457100550551416)
XLA Ops:
  0.6 0.0 copy-start.4
  0.6 0.0 copy-start.5
  0.7 0.6 copy-done.4
  1.3 0.0 copy-done.5
  1.3 0.0 copy-start
  1.3 0.9 %copy-done = bf16[3,3,64,64]{3,2,1,0:T(8,128)(2,1)S(1)} copy-done((bf16[3,3,64,64]{3,2,1,0:T(8,128)(2,1)S(1)}, bf16[3,3,64,64]{3,2,1,0:T(8,128)(2,1)}, u32[]{:S(2)}) %copy-start) | copy-done | bytes 73752
  2.2 0.0 copy-start.1
  2.2 0.9 %copy-done.1 = bf16[3,3,64,64]{3,2,1,0:T(8,128)(2,1)S(1)} copy-done((bf16[3,3,64,64]{3,2,1,0:T(8,128)(2,1)S(1)}, bf16[3,3,64,64]{3,2,1,0:T(8,128)(2,1)}, u32[]{:S(2)}) %copy-start.1) | copy-done | bytes 73752
  3.1 0.0 copy-start.2
  3.1 0.8 %copy-done.2 = bf16[32,1024]{1,0:T(8,128)(2,1)S(1)} copy-done((bf16[32,1024]{1,0:T(8,128)(2,1)S(1)}, bf16[32,1024]{1,0:T(8,128)(2,1)}, u32[]{:S(2)}) %copy-start.2) | copy-done | bytes 65560
  4.0 0.0 copy-start.3
  4.0 0.8 %copy-done.3 = bf16[32,1024]{1,0:T(8,128)(2,1)S(1)} copy-done((bf16[32,1024]{1,0:T(8,128)(2,1)S(1)}, bf16[32,1024]{1,0:T(8,128)(2,1)}, u32[]{:S(2)}) %copy-start.3) | copy-done | bytes 65560
  4.8 63.6 %shard_map.109 = (bf16[32,1024]{1,0:T(8,128)(2,1)S(1)}, bf16[32,1024]{1,0:T(8,128)(2,1)S(1)}, f32[64,10,128]{2,1,0:T(8,128)S(1)}) custom-call(bf16[32,1024]{1,0:T(8,128)(2,1)S(1)} %copy-done.2, bf16[32,1024]{1,0:T(8,128)(2,1)S(1)} %copy-done.3, bf16[3,3,64,64]{3,2,1,0:T(8,128)(2,1)S(1)} %copy-done, bf16[3,3,64,64]{3,2,1,0:T(8,128)(2,1)S(1)} %copy-done.1, ...), custom_call_target="tpu_custom_call" | custom-call | tf_op jit(solution)/shard_map/pallas_call | solution.py:362
  68.4 0.1 slice_reduce_fusion
  68.5 0.1 copy.14
  68.6 0.6 fusion.1
  69.2 0.9 %fusion = (f32[3,3,64,64]{3,2,1,0:T(8,128)}, f32[3,3,64,64]{3,2,1,0:T(8,128)}) fusion(f32[3,3,64,128]{3,2,1,0:T(8,128)S(1)} %bitcast.7), kind=kLoop, calls=%fused_computation.2 | loop fusion | bytes 589824 | tf_op jit(solution)/shard_map/slice | solution.py:392
  70.1 0.6 copy.17
  70.7 0.6 copy.18
  (1 shorter events, 0.0 us)
Async XLA Ops:
  0.6 0.7 copy-start.4
  0.6 0.7 copy-start.5
  1.3 0.9 %copy-start = (bf16[3,3,64,64]{3,2,1,0:T(8,128)(2,1)S(1)}, bf16[3,3,64,64]{3,2,1,0:T(8,128)(2,1)}, u32[]{:S(2)}) copy-start(bf16[3,3,64,64]{3,2,1,0:T(8,128)(2,1)} %one_hbm.1) | copy-start | bytes 221188
  2.2 0.9 %copy-start.1 = (bf16[3,3,64,64]{3,2,1,0:T(8,128)(2,1)S(1)}, bf16[3,3,64,64]{3,2,1,0:T(8,128)(2,1)}, u32[]{:S(2)}) copy-start(bf16[3,3,64,64]{3,2,1,0:T(8,128)(2,1)} %two_hbm.1) | copy-start | bytes 221188
  3.1 0.8 %copy-start.2 = (bf16[32,1024]{1,0:T(8,128)(2,1)S(1)}, bf16[32,1024]{1,0:T(8,128)(2,1)}, u32[]{:S(2)}) copy-start(bf16[32,1024]{1,0:T(8,128)(2,1)} %act_hbm.1) | copy-start | bytes 196612
  4.0 0.8 %copy-start.3 = (bf16[32,1024]{1,0:T(8,128)(2,1)S(1)}, bf16[32,1024]{1,0:T(8,128)(2,1)}, u32[]{:S(2)}) copy-start(bf16[32,1024]{1,0:T(8,128)(2,1)} %cot_hbm.1) | copy-start | bytes 196612

commit v3 on v2

--- a/solution.py
+++ b/solution.py
@@ -142,12 +142,12 @@
 
 
 def kernel(
-    act_hbm, cot_hbm, one_hbm, two_hbm, bias_one, bias_two,
+    act_hbm, cot_hbm, one_hbm, two_hbm, bias_one_hbm, bias_two_hbm,
     sym_out, grad_out, full,
-    act, cot, one, two, mat_one, mat_two, back_one, back_two,
-    source_pad, sym_pad, mirror, summed, mirror_sum, spare,
-    parts, core_in, plane_in, depth_in, piece,
-    load_sem, m_send, m_recv, s_send, s_recv, x_send, x_recv, g_send, g_recv, ar_send, ar_recv,
+    act, cot, one, two, bias_one, bias_two, mat_one, mat_two, back_one, back_two,
+    source_pad, sym_pad, mirror, summed, relay, mirror_sum, spare,
+    parts, core_in, plane_in, depth_in,
+    load_sem, m_send, m_recv, s_send, s_recv, r_send, r_recv, x_send, x_recv, g_send, g_recv, ar_send, ar_recv,
 ):
     row, col = lax.axis_index("row"), lax.axis_index("col")
     core = lax.rem(col, 2)
@@ -177,7 +177,9 @@
 
     loads = [
         pltpu.make_async_copy(src, dst, load_sem.at[k])
-        for k, (src, dst) in enumerate(((act_hbm, act), (one_hbm, one), (two_hbm, two), (cot_hbm, cot)))
+        for k, (src, dst) in enumerate((
+            (act_hbm, act), (one_hbm, one), (two_hbm, two), (cot_hbm, cot), (bias_one_hbm, bias_one), (bias_two_hbm, bias_two)
+        ))
     ]
     for copy in loads:
         copy.start()
@@ -220,8 +222,8 @@
     swap_start(cot_hbm, mirror, m_send, m_recv)
     source_halo = halo_start(source_pad, s_send, s_recv)
 
-    loads[1].wait()
-    loads[2].wait()
+    for copy in loads[1:]:
+        copy.wait()
     fill(mat_one, one, False)
     fill(mat_two, two, False)
     fill(back_two, two, True)
@@ -255,14 +257,18 @@
     branch = conv(hidden_groups, mat_two, 32) + wide_two
     summed[...] = (source + jnp.concatenate([branch[g] for g in range(4)], axis=1)).astype(BF16)
 
-    loads[3].wait()
+    for step in range(1, DEPTH):
+        pltpu.make_async_remote_copy(
+            src_ref=summed.at[:, pl.ds(128 * step, 128)], dst_ref=relay.at[depth], send_sem=r_send, recv_sem=r_recv,
+            device_id=depth_id(row, col, lax.rem(depth + step, DEPTH)), device_id_type=MESH,
+        ).start()
+    relay[depth] = summed[:, 0:128]
     for h in range(2):
         pltpu.make_async_copy(mirror.at[h], mirror.at[h], m_recv.at[h]).wait()
     turned_cot = jnp.concatenate([turned(mirror[h].astype(F32), spare, 256 * h) for h in range(2)], axis=0)
     sym = ((cot[...].astype(F32) + turned_cot) * 0.5).astype(BF16).astype(F32)
     pack(sym, sym_pad)
     sym_halo = halo_start(sym_pad, g_send, g_recv)
-    swap_start(summed, mirror_sum, x_send, x_recv)
 
     sym_own = grouped(sym)
     lower = jnp.zeros((4, 8, QUAD), F32)
@@ -304,6 +310,26 @@
             device_id=plane_id(row, col, peer), device_id_type=MESH,
         ).start()
 
+    pltpu.make_async_copy(relay.at[pl.ds(0, DEPTH - 1)], relay.at[pl.ds(0, DEPTH - 1)], r_recv).wait()
+
+    @pl.loop(0, DEPTH)
+    def _(origin):
+        lanes = pl.ds(pl.multiple_of(128 * lax.rem(depth - origin + DEPTH, DEPTH), 128), 128)
+        for h in range(2):
+            src, dst = relay.at[origin, pl.ds(16 * h, 16)], mirror_sum.at[core, :, lanes]
+            here = is_self[h] & (origin == depth)
+
+            @pl.when(jnp.logical_not(here))
+            def _():
+                pltpu.make_async_remote_copy(
+                    src_ref=src, dst_ref=dst, send_sem=x_send, recv_sem=x_recv,
+                    device_id=(col // 2, 2 * (row - depth + origin) + h), device_id_type=MESH,
+                ).start()
+
+            @pl.when(here)
+            def _():
+                pltpu.make_async_copy(src, dst, x_recv).start()
+
     for copy in sym_halo:
         copy.wait_recv()
     clear_edges(sym_pad, row, col)
@@ -323,11 +349,6 @@
             device_id=depth_id(row, col, peer), device_id_type=MESH,
         ).start()
 
-    for h in range(2):
-        pltpu.make_async_copy(mirror_sum.at[h], mirror_sum.at[h], x_recv.at[h]).wait()
-    turned_sum = jnp.concatenate([turned(mirror_sum[h].astype(F32), spare, 256 * h) for h in range(2)], axis=0)
-    sym_out[...] = ((summed[...].astype(F32) + turned_sum) * 0.5).astype(BF16)
-
     pltpu.make_async_copy(depth_in.at[pl.ds(0, DEPTH - 1)], depth_in.at[pl.ds(0, DEPTH - 1)], ar_recv.at[2]).wait()
     here = PLANE * core + plane
     full[here] = jnp.sum(depth_in[...], axis=0) * INV_BINS
@@ -345,8 +366,23 @@
         device_id=sibling, device_id_type=MESH,
     )
     back_core.start()
+    pltpu.make_async_copy(mirror_sum, mirror_sum, x_recv).wait()
+    turned_sum = jnp.concatenate([turned(mirror_sum[h].astype(F32), spare, 256 * h) for h in range(2)], axis=0)
+    sym_out[...] = ((summed[...].astype(F32) + turned_sum) * 0.5).astype(BF16)
+
     swap_sent(cot_hbm, mirror, m_send)
-    swap_sent(summed, mirror_sum, x_send)
+    pltpu.make_async_copy(relay.at[pl.ds(0, DEPTH - 1)], relay.at[pl.ds(0, DEPTH - 1)], r_send).wait()
+
+    @pl.when(jnp.logical_not(diagonal))
+    def _():
+        pltpu.make_async_copy(mirror_sum, mirror_sum, x_send).wait()
+
+    @pl.when(diagonal)
+    def _():
+        piece = mirror_sum.at[0, :, pl.ds(0, 7 * 128)]
+        pltpu.make_async_copy(mirror_sum.at[1], mirror_sum.at[1], x_send).wait()
+        pltpu.make_async_copy(piece, piece, x_send).wait()
+
     for copy in source_halo + sym_halo + [to_core]:
         copy.wait_send()
     pltpu.make_async_copy(plane_in, plane_in, ar_send.at[1]).wait()
@@ -355,20 +391,43 @@
     back_core.wait()
 
 
+def unfold(sym, grad, full, sym_out, grad_out, one_out, bias_one_out, two_out, bias_two_out, sems):
+    copies = [pltpu.make_async_copy(sym, sym_out, sems.at[0]), pltpu.make_async_copy(grad, grad_out, sems.at[1])]
+    for copy in copies:
+        copy.start()
+    for a in range(3):
+        for b in range(3):
+            tap = full[:, 3 * a + b, :]
+            one_out[a, b] = tap[:, :CH]
+            two_out[a, b] = pltpu.roll(tap, CH, 1)[:, :CH]
+    bias = jnp.sum(full[:, 9, :], axis=0, keepdims=True)
+    bias_one_out[...] = bias[:, :CH]
+    bias_two_out[...] = pltpu.roll(bias, CH, 1)[:, :CH]
+    for copy in copies:
+        copy.wait()
+
+
 def on_device(activations, conv_one, bias_one, conv_two, bias_two, cotangent):
     vmem, anywhere = pl.BlockSpec(memory_space=pltpu.VMEM), pl.BlockSpec(memory_space=pl.ANY)
     dma = pltpu.SemaphoreType.DMA
     tile = jax.ShapeDtypeStruct((ROWS, WIDTH), BF16)
-    symmetric_out, input_grad, full = pl.pallas_call(
+    inputs = (activations, cotangent, conv_one, conv_two, bias_one.reshape(1, CH), bias_two.reshape(1, CH))
+    held = pl.pallas_call(
         kernel,
-        out_shape=(tile, tile, jax.ShapeDtypeStruct((CH, LINES, 128), F32)),
-        in_specs=[anywhere] * 4 + [vmem] * 2,
+        out_shape=(
+            pltpu.VMEM((ROWS, WIDTH), BF16),
+            pltpu.VMEM((ROWS, WIDTH), BF16),
+            pltpu.VMEM((CH, LINES, 128), F32),
+        ),
+        in_specs=[anywhere] * 6,
         out_specs=[vmem] * 3,
         scratch_shapes=[
             pltpu.VMEM((ROWS, WIDTH), BF16),
             pltpu.VMEM((ROWS, WIDTH), BF16),
             pltpu.VMEM((3, 3, CH, CH), BF16),
             pltpu.VMEM((3, 3, CH, CH), BF16),
+            pltpu.VMEM((1, CH), F32),
+            pltpu.VMEM((1, CH), F32),
         ]
         + [pltpu.VMEM((3 * QUAD, 3 * QUAD), BF16)] * 4
         + [
@@ -376,20 +435,28 @@
             pltpu.VMEM((6, 4, 16, QUAD), BF16),
             pltpu.VMEM((2, 16, WIDTH), BF16),
             pltpu.VMEM((ROWS, WIDTH), BF16),
+            pltpu.VMEM((DEPTH, ROWS, 128), BF16),
             pltpu.VMEM((2, 16, WIDTH), BF16),
             pltpu.VMEM((512, 128), F32),
             pltpu.VMEM((CH, LINES, 128), F32),
             pltpu.VMEM((PLANE, LINES, 128), F32),
             pltpu.VMEM((PLANE - 1, LINES, 128), F32),
             pltpu.VMEM((DEPTH, LINES, 128), F32),
-            pltpu.VMEM((LINES, 128), F32),
-            dma((4,)), dma((2,)), dma((2,)), dma((8,)), dma((8,)), dma((2,)), dma((2,)), dma((8,)), dma((8,)), dma((5,)), dma((5,)),
+            dma((6,)), dma((2,)), dma((2,)), dma((8,)), dma((8,)), dma, dma, dma, dma, dma((8,)), dma((8,)), dma((5,)), dma((5,)),
         ],
         compiler_params=pltpu.CompilerParams(collective_id=0, has_side_effects=True, vmem_limit_bytes=48 * 1024 * 1024),
-    )(activations, cotangent, conv_one, conv_two, bias_one.reshape(1, CH), bias_two.reshape(1, CH))
-    taps = jnp.swapaxes(full[:, :9], 0, 1).reshape(3, 3, CH, 2 * CH)
-    biases = jnp.sum(full[:, 9], axis=0)
-    return symmetric_out, input_grad, taps[..., :CH], biases[:CH], taps[..., CH:], biases[CH:]
+    )(*(pltpu.with_memory_space_constraint(x, pltpu.HBM) for x in inputs))
+    taps = jax.ShapeDtypeStruct((3, 3, CH, CH), F32)
+    bias = jax.ShapeDtypeStruct((1, CH), F32)
+    symmetric_out, input_grad, grad_w1, grad_b1, grad_w2, grad_b2 = pl.pallas_call(
+        unfold,
+        out_shape=(tile, tile, taps, bias, taps, bias),
+        in_specs=[vmem] * 3,
+        out_specs=[anywhere] * 2 + [vmem] * 4,
+        scratch_shapes=[dma((2,))],
+        compiler_params=pltpu.CompilerParams(vmem_limit_bytes=8 * 1024 * 1024),
+    )(*(pltpu.with_memory_space_constraint(x, pltpu.VMEM) for x in held))
+    return symmetric_out, input_grad, grad_w1, grad_b1.reshape(CH), grad_w2, grad_b2.reshape(CH)
 
 
 def solution(mesh):

time: 71.6 us -> 56.6 us (0.79)
  Pallas kernels: 63.6 us -> 55.8 us
  local copies, waits for them, and re-layouts: 7.02 us -> 0 us
    pallas_call x1 -> x2, Pallas kernels: 63.6 us -> 55.8 us  [the longest x1 54.2 us: on_device(): pl.pallas_call(kernel, out_shape=(pltpu.VMEM((ROWS, WIDTH), BF16), pltpu....]
    unnamed x14 -> x0, local copies, waits for them, and re-layouts: 5.41 us -> none
    slice x2 -> x0, local copies, waits for them, and re-layouts: 1.48 us -> none  [the longest x1 0.9 us: on_device(): taps[..., CH:]]
where the time goes in v3:
time: 56.6 us; the launch traced here: 56.5 us
  Pallas kernels  55.8 us (99%)
  between operations  0.64 us (1%)
    pallas_call x1, Pallas kernels, on_device(): pl.pallas_call(kernel, out_shape=(pltpu.VMEM((ROWS, WIDTH), BF16), pltpu....  54.2 us
    pallas_call x1, Pallas kernels, on_device(): pl.pallas_call(unfold, out_shape=(tile, tile, taps, bias, taps, bias), in...  1.67 us

profile of v3, /device:TPU:1, one launch (start us, length us, event | category | flops | bytes accessed | tf_op | source)
XLA Modules:
  0.0 56.5 jit_solution(14476139857352963901)
XLA Ops:
  0.6 54.2 %shard_map.109 = (bf16[32,1024]{1,0:T(8,128)(2,1)S(1)}, bf16[32,1024]{1,0:T(8,128)(2,1)S(1)}, f32[64,10,128]{2,1,0:T(8,128)S(1)}) custom-call(bf16[32,1024]{1,0:T(8,128)(2,1)} %act_hbm.1, bf16[32,1024]{1,0:T(8,128)(2,1)} %cot_hbm.1, bf16[3,3,64,64]{3,2,1,0:T(8,128)(2,1)} %one_hbm.1, bf16[3,3,64,64]{3,2,1,0:T(8,128)(2,1)} %two_hbm.1, f32[1,64]{1,0:T(1,128)} %bitcast.4, ...), custom_call_target="tpu_custom_call" | custom-call | tf_op jit(solution)/shard_map/pallas_call | solution.py:415
  54.8 1.7 %shard_map.110 = (bf16[32,1024]{1,0:T(8,128)(2,1)}, bf16[32,1024]{1,0:T(8,128)(2,1)}, f32[3,3,64,64]{3,2,1,0:T(8,128)}, f32[1,64]{1,0:T(1,128)}, f32[3,3,64,64]{3,2,1,0:T(8,128)}, /*index=5*/f32[1,64]{1,0:T(1,128)}) custom-call(bf16[32,1024]{1,0:T(8,128)(2,1)S(1)} %get-tuple-element.15.sym, bf16[32,1024]{1,0:T(8,128)(2,1)S(1)} %get-tuple-element.16.grad, ...), custom_call_target="tpu_custom_call" | custom-call | tf_op jit(solution)/shard_map/pallas_call | solution.py:451

commit v4 on v3

--- a/solution.py
+++ b/solution.py
@@ -66,7 +66,7 @@
 def unpack(padded):
     values = padded[...].astype(F32)
     return [
-        jnp.concatenate([values[q, g // 2, 8 * (g % 2) : 8 * (g % 2) + 8] for q in range(6)], axis=0).astype(BF16)
+        jnp.concatenate([values[q, g // 2, 8 * (g % 2) : 8 * (g % 2) + 8] for q in range(6)], axis=0)
         for g in range(8)
     ]
 
@@ -91,6 +91,7 @@
 
 def conv(groups, matrix, rows):
     count = len(groups) - 2
+    groups = [group.astype(BF16) for group in groups]
     left = jnp.concatenate([jnp.stack(groups[b : b + count]) for b in range(3)], axis=-1)
     full = jnp.dot(left.reshape(count * 48, 3 * QUAD), matrix[...], preferred_element_type=F32)
     full = full.reshape(count, 48, 3 * QUAD)
@@ -101,27 +102,34 @@
     )
 
 
-def taps_of(groups, grads):
-    count, rows = grads.shape[:2]
-    shifted = []
+def spread(own, matrix):
+    left = own.reshape(128, QUAD).astype(BF16)
+    columns = []
+    for b in range(3):
+        full = jnp.dot(left, matrix[b * QUAD : (b + 1) * QUAD], preferred_element_type=F32).reshape(4, 32, 3 * QUAD)
+        lower, upper = jnp.zeros((4, 4, QUAD), F32), jnp.zeros((4, 8, QUAD), F32)
+        columns.append(
+            jnp.concatenate([upper, full[:, :, :QUAD]], axis=1)
+            + jnp.concatenate([lower, full[:, :, QUAD : 2 * QUAD], lower], axis=1)
+            + jnp.concatenate([full[:, :, 2 * QUAD :], upper], axis=1)
+        )
+    out = []
+    for g in range(6):
+        terms = [columns[b][g - 2 + b] for b in range(3) if 0 <= g - 2 + b < 4]
+        out.append(sum(terms[1:], terms[0]))
+    return jnp.stack(out)
+
+
+def windows(groups, count, rows, turned_rows):
     for a in range(3):
-        parts = [grads]
-        if a:
-            parts.insert(0, jnp.zeros((count, 4 * a, QUAD), F32))
-        if 48 - rows - 4 * a:
-            parts.append(jnp.zeros((count, 48 - rows - 4 * a, QUAD), F32))
-        shifted.append(jnp.concatenate(parts, axis=1) if len(parts) > 1 else grads)
-    right = jnp.concatenate(shifted, axis=-1).astype(BF16).reshape(count * 48, 3 * QUAD)
-    out = []
-    for b in range(3):
-        left = jnp.stack(groups[b : b + count]).reshape(count * 48, QUAD)
-        out.append(lax.dot_general(left, right, (((0,), (0,)), ((), ())), preferred_element_type=F32))
-    return out
-
-
-def halves(full, a):
-    one = full[:, a * QUAD : a * QUAD + 128]
-    two = full[:, a * QUAD + 128 : (a + 1) * QUAD]
+        for b in range(3):
+            window = jnp.concatenate([groups[g][4 * a : 4 * a + rows] for g in range(b, b + count)], axis=0)
+            turned_rows[pl.ds(QUAD * (3 * a + b), QUAD), 0 : count * rows] = window.astype(BF16).T
+
+
+def halves(full, tap):
+    one = full[tap * QUAD : (tap + 1) * QUAD, :128]
+    two = full[tap * QUAD : (tap + 1) * QUAD, 128:]
     return one[0:64] + two[128:192], one[64:128] + two[192:256]
 
 
@@ -146,7 +154,7 @@
     sym_out, grad_out, full,
     act, cot, one, two, bias_one, bias_two, mat_one, mat_two, back_one, back_two,
     source_pad, sym_pad, mirror, summed, relay, mirror_sum, spare,
-    parts, core_in, plane_in, depth_in,
+    hidden_turned, source_turned, parts, core_in, plane_in, depth_in,
     load_sem, m_send, m_recv, s_send, s_recv, r_send, r_recv, x_send, x_recv, g_send, g_recv, ar_send, ar_recv,
 ):
     row, col = lax.axis_index("row"), lax.axis_index("col")
@@ -159,22 +167,6 @@
     diagonal = col // 2 == row
     is_self = [diagonal & (core == h) for h in range(2)]
 
-    barrier = pltpu.get_barrier_semaphore()
-    for h in range(2):
-        @pl.when(jnp.logical_not(is_self[h]))
-        def _():
-            pl.semaphore_signal(barrier, inc=1, device_id=opposite[h], device_id_type=MESH)
-    for device in around + [sibling]:
-        pl.semaphore_signal(barrier, inc=1, device_id=device, device_id_type=MESH)
-
-    @pl.loop(1, PLANE)
-    def _(step):
-        pl.semaphore_signal(barrier, inc=1, device_id=plane_id(row, col, lax.rem(plane + step, PLANE)), device_id_type=MESH)
-
-    @pl.loop(1, DEPTH)
-    def _(step):
-        pl.semaphore_signal(barrier, inc=1, device_id=depth_id(row, col, lax.rem(depth + step, DEPTH)), device_id_type=MESH)
-
     loads = [
         pltpu.make_async_copy(src, dst, load_sem.at[k])
         for k, (src, dst) in enumerate((
@@ -183,6 +175,22 @@
     ]
     for copy in loads:
         copy.start()
+    barrier = pltpu.get_barrier_semaphore()
+    for h in range(2):
+        @pl.when(jnp.logical_not(is_self[h]))
+        def _():
+            pl.semaphore_signal(barrier, inc=1, device_id=opposite[h], device_id_type=MESH)
+    for device in around + [sibling]:
+        pl.semaphore_signal(barrier, inc=1, device_id=device, device_id_type=MESH)
+
+    @pl.loop(1, PLANE)
+    def _(step):
+        pl.semaphore_signal(barrier, inc=1, device_id=plane_id(row, col, lax.rem(plane + step, PLANE)), device_id_type=MESH)
+
+    @pl.loop(1, DEPTH)
+    def _(step):
+        pl.semaphore_signal(barrier, inc=1, device_id=depth_id(row, col, lax.rem(depth + step, DEPTH)), device_id_type=MESH)
+
     loads[0].wait()
     source = act[...].astype(F32)
     pack(source, source_pad)
@@ -218,12 +226,13 @@
             copies[-1].start()
         return copies
 
+    loads[3].wait()
     pl.semaphore_wait(barrier, 2 + 8 + 1 + PLANE - 1 + DEPTH - 1 - diagonal.astype(jnp.int32))
-    swap_start(cot_hbm, mirror, m_send, m_recv)
+    swap_start(cot, mirror, m_send, m_recv)
     source_halo = halo_start(source_pad, s_send, s_recv)
 
-    for copy in loads[1:]:
-        copy.wait()
+    for k in (1, 2, 4, 5):
+        loads[k].wait()
     fill(mat_one, one, False)
     fill(mat_two, two, False)
     fill(back_two, two, True)
@@ -252,7 +261,7 @@
         + 0.5 * preact * (1.0 - bent * bent) * (SLOPE * (1.0 + 3.0 * CUBIC * preact * preact))
     )
     blank = jnp.zeros((6, 8, QUAD), F32)
-    hidden = jnp.concatenate([hidden, blank], axis=1).astype(BF16)
+    hidden = jnp.concatenate([hidden, blank], axis=1)
     hidden_groups = [hidden[g] for g in range(6)]
     branch = conv(hidden_groups, mat_two, 32) + wide_two
     summed[...] = (source + jnp.concatenate([branch[g] for g in range(4)], axis=1)).astype(BF16)
@@ -263,26 +272,24 @@
             device_id=depth_id(row, col, lax.rem(depth + step, DEPTH)), device_id_type=MESH,
         ).start()
     relay[depth] = summed[:, 0:128]
+    windows(hidden_groups, 4, 32, hidden_turned)
+    windows(source_groups, 6, 40, source_turned)
+    source_turned[:, 240:QUAD] = jnp.zeros((9 * QUAD, 16), BF16)
     for h in range(2):
         pltpu.make_async_copy(mirror.at[h], mirror.at[h], m_recv.at[h]).wait()
     turned_cot = jnp.concatenate([turned(mirror[h].astype(F32), spare, 256 * h) for h in range(2)], axis=0)
     sym = ((cot[...].astype(F32) + turned_cot) * 0.5).astype(BF16).astype(F32)
-    pack(sym, sym_pad)
-    sym_halo = halo_start(sym_pad, g_send, g_recv)
 
     sym_own = grouped(sym)
-    lower = jnp.zeros((4, 8, QUAD), F32)
-    sym_rows = jnp.concatenate([lower, sym_own, lower], axis=1).astype(BF16)
-    nothing = jnp.zeros((48, QUAD), BF16)
-    sym_groups = [nothing] * 2 + [sym_rows[g] for g in range(4)] + [nothing] * 2
-    share = conv(sym_groups, back_two, 40) * slope
-    taps_two = taps_of(hidden_groups, sym_own)
-    taps_one = taps_of(source_groups, share)
+    share = spread(sym_own, back_two) * slope
+    taps_two = jnp.dot(hidden_turned[...], sym_own.reshape(128, QUAD).astype(BF16), preferred_element_type=F32)
+    rows = jnp.concatenate([share.reshape(240, QUAD), jnp.zeros((16, QUAD), F32)], axis=0).astype(BF16)
+    taps_one = jnp.dot(source_turned[...], rows, preferred_element_type=F32)
     left = lax.broadcasted_iota(jnp.int32, (CH, 128), 1) < CH
     for a in range(3):
         for b in range(3):
-            near_one, far_one = halves(taps_one[b], a)
-            near_two, far_two = halves(taps_two[b], a)
+            near_one, far_one = halves(taps_one, 3 * a + b)
+            near_two, far_two = halves(taps_two, 3 * a + b)
             parts[:, 3 * a + b, :] = jnp.where(
                 left, near_one + pltpu.roll(far_one, CH, 1), far_two + pltpu.roll(near_two, CH, 1)
             )
@@ -299,6 +306,8 @@
         device_id=sibling, device_id_type=MESH,
     )
     to_core.start()
+    pack(sym, sym_pad)
+    sym_halo = halo_start(sym_pad, g_send, g_recv)
     to_core.wait_recv()
     core_in[...] = core_in[...] + parts[own]
 
@@ -330,6 +339,28 @@
             def _():
                 pltpu.make_async_copy(src, dst, x_recv).start()
 
+    pltpu.make_async_copy(plane_in, plane_in, ar_recv.at[1]).wait()
+    depth_in[depth] = jnp.sum(plane_in[...], axis=0) + core_in[plane]
+
+    @pl.loop(1, DEPTH)
+    def _(step):
+        peer = lax.rem(depth + step, DEPTH)
+        pltpu.make_async_remote_copy(
+            src_ref=depth_in.at[depth], dst_ref=depth_in.at[depth], send_sem=ar_send.at[2], recv_sem=ar_recv.at[2],
+            device_id=depth_id(row, col, peer), device_id_type=MESH,
+        ).start()
+
+    pltpu.make_async_copy(depth_in.at[pl.ds(0, DEPTH - 1)], depth_in.at[pl.ds(0, DEPTH - 1)], ar_recv.at[2]).wait()
+    here = PLANE * core + plane
+    full[here] = jnp.sum(depth_in[...], axis=0) * INV_BINS
+
+    @pl.loop(1, PLANE)
+    def _(step):
+        pltpu.make_async_remote_copy(
+            src_ref=full.at[here], dst_ref=full.at[here], send_sem=ar_send.at[3], recv_sem=ar_recv.at[3],
+            device_id=plane_id(row, col, lax.rem(plane + step, PLANE)), device_id_type=MESH,
+        ).start()
+
     for copy in sym_halo:
         copy.wait_recv()
     clear_edges(sym_pad, row, col)
@@ -337,28 +368,6 @@
     pre_grad = jnp.concatenate([pre_grad, blank], axis=1).astype(BF16)
     input_grad = conv([pre_grad[g] for g in range(6)], back_one, 32)
     grad_out[...] = (sym + jnp.concatenate([input_grad[g] for g in range(4)], axis=1)).astype(BF16)
-
-    pltpu.make_async_copy(plane_in, plane_in, ar_recv.at[1]).wait()
-    depth_in[depth] = jnp.sum(plane_in[...], axis=0) + core_in[plane]
-
-    @pl.loop(1, DEPTH)
-    def _(step):
-        peer = lax.rem(depth + step, DEPTH)
-        pltpu.make_async_remote_copy(
-            src_ref=depth_in.at[depth], dst_ref=depth_in.at[depth], send_sem=ar_send.at[2], recv_sem=ar_recv.at[2],
-            device_id=depth_id(row, col, peer), device_id_type=MESH,
-        ).start()
-
-    pltpu.make_async_copy(depth_in.at[pl.ds(0, DEPTH - 1)], depth_in.at[pl.ds(0, DEPTH - 1)], ar_recv.at[2]).wait()
-    here = PLANE * core + plane
-    full[here] = jnp.sum(depth_in[...], axis=0) * INV_BINS
-
-    @pl.loop(1, PLANE)
-    def _(step):
-        pltpu.make_async_remote_copy(
-            src_ref=full.at[here], dst_ref=full.at[here], send_sem=ar_send.at[3], recv_sem=ar_recv.at[3],
-            device_id=plane_id(row, col, lax.rem(plane + step, PLANE)), device_id_type=MESH,
-        ).start()
 
     pltpu.make_async_copy(plane_in, plane_in, ar_recv.at[3]).wait()
     back_core = pltpu.make_async_remote_copy(
@@ -370,7 +379,7 @@
     turned_sum = jnp.concatenate([turned(mirror_sum[h].astype(F32), spare, 256 * h) for h in range(2)], axis=0)
     sym_out[...] = ((summed[...].astype(F32) + turned_sum) * 0.5).astype(BF16)
 
-    swap_sent(cot_hbm, mirror, m_send)
+    swap_sent(cot, mirror, m_send)
     pltpu.make_async_copy(relay.at[pl.ds(0, DEPTH - 1)], relay.at[pl.ds(0, DEPTH - 1)], r_send).wait()
 
     @pl.when(jnp.logical_not(diagonal))
@@ -391,18 +400,23 @@
     back_core.wait()
 
 
-def unfold(sym, grad, full, sym_out, grad_out, one_out, bias_one_out, two_out, bias_two_out, sems):
-    copies = [pltpu.make_async_copy(sym, sym_out, sems.at[0]), pltpu.make_async_copy(grad, grad_out, sems.at[1])]
-    for copy in copies:
+def unfold(sym, grad, full, sym_out, grad_out, one_out, bias_one_out, two_out, bias_two_out, one, two, bias_one, bias_two, sems):
+    def send(k, src, dst):
+        copy = pltpu.make_async_copy(src, dst, sems.at[k])
         copy.start()
+        return copy
+
+    copies = [send(0, sym, sym_out), send(1, grad, grad_out)]
+    bias = jnp.sum(full[:, 9, :], axis=0, keepdims=True)
+    bias_one[...] = bias[:, :CH]
+    bias_two[...] = pltpu.roll(bias, CH, 1)[:, :CH]
+    copies += [send(2, bias_one, bias_one_out), send(3, bias_two, bias_two_out)]
     for a in range(3):
         for b in range(3):
             tap = full[:, 3 * a + b, :]
-            one_out[a, b] = tap[:, :CH]
-            two_out[a, b] = pltpu.roll(tap, CH, 1)[:, :CH]
-    bias = jnp.sum(full[:, 9, :], axis=0, keepdims=True)
-    bias_one_out[...] = bias[:, :CH]
-    bias_two_out[...] = pltpu.roll(bias, CH, 1)[:, :CH]
+            one[a, b] = tap[:, :CH]
+            two[a, b] = pltpu.roll(tap, CH, 1)[:, :CH]
+        copies += [send(4 + a, one.at[a], one_out.at[a]), send(7 + a, two.at[a], two_out.at[a])]
     for copy in copies:
         copy.wait()
 
@@ -438,6 +452,8 @@
             pltpu.VMEM((DEPTH, ROWS, 128), BF16),
             pltpu.VMEM((2, 16, WIDTH), BF16),
             pltpu.VMEM((512, 128), F32),
+            pltpu.VMEM((9 * QUAD, 128), BF16),
+            pltpu.VMEM((9 * QUAD, QUAD), BF16),
             pltpu.VMEM((CH, LINES, 128), F32),
             pltpu.VMEM((PLANE, LINES, 128), F32),
             pltpu.VMEM((PLANE - 1, LINES, 128), F32),
@@ -452,8 +468,8 @@
         unfold,
         out_shape=(tile, tile, taps, bias, taps, bias),
         in_specs=[vmem] * 3,
-        out_specs=[anywhere] * 2 + [vmem] * 4,
-        scratch_shapes=[dma((2,))],
+        out_specs=[anywhere] * 6,
+        scratch_shapes=[pltpu.VMEM((3, 3, CH, CH), F32)] * 2 + [pltpu.VMEM((1, CH), F32)] * 2 + [dma((10,))],
         compiler_params=pltpu.CompilerParams(vmem_limit_bytes=8 * 1024 * 1024),
     )(*(pltpu.with_memory_space_constraint(x, pltpu.VMEM) for x in held))
     return symmetric_out, input_grad, grad_w1, grad_b1.reshape(CH), grad_w2, grad_b2.reshape(CH)

time: 56.6 us -> 55.4 us (0.979)
  Pallas kernels: 55.8 us -> 54.6 us
    pallas_call x1, Pallas kernels: 54.2 us -> 53.5 us  [on_device(): pl.pallas_call(kernel, out_shape=(pltpu.VMEM((ROWS, WIDTH), BF16), pltpu....]
where the time goes in v4:
time: 55.4 us; the launch traced here: 55.3 us
  Pallas kernels  54.6 us (99%)
  between operations  0.64 us (1%)
    pallas_call x1, Pallas kernels, on_device(): pl.pallas_call(kernel, out_shape=(pltpu.VMEM((ROWS, WIDTH), BF16), pltpu....  53.5 us

profile of v4, /device:TPU:1, one launch (start us, length us, event | category | flops | bytes accessed | tf_op | source)
XLA Modules:
  0.0 55.3 jit_solution(15881947946718664906)
XLA Ops:
  0.6 53.5 %shard_map.109 = (bf16[32,1024]{1,0:T(8,128)(2,1)S(1)}, bf16[32,1024]{1,0:T(8,128)(2,1)S(1)}, f32[64,10,128]{2,1,0:T(8,128)S(1)}) custom-call(bf16[32,1024]{1,0:T(8,128)(2,1)} %act_hbm.1, bf16[32,1024]{1,0:T(8,128)(2,1)} %cot_hbm.1, bf16[3,3,64,64]{3,2,1,0:T(8,128)(2,1)} %one_hbm.1, bf16[3,3,64,64]{3,2,1,0:T(8,128)(2,1)} %two_hbm.1, f32[1,64]{1,0:T(1,128)} %bitcast.4, ...), custom_call_target="tpu_custom_call" | custom-call | tf_op jit(solution)/shard_map/pallas_call | solution.py:429
  54.2 1.1 %shard_map.110 = (bf16[32,1024]{1,0:T(8,128)(2,1)}, bf16[32,1024]{1,0:T(8,128)(2,1)}, f32[3,3,64,64]{3,2,1,0:T(8,128)}, f32[1,64]{1,0:T(1,128)}, f32[3,3,64,64]{3,2,1,0:T(8,128)}, /*index=5*/f32[1,64]{1,0:T(1,128)}) custom-call(bf16[32,1024]{1,0:T(8,128)(2,1)S(1)} %get-tuple-element.15.sym, bf16[32,1024]{1,0:T(8,128)(2,1)S(1)} %get-tuple-element.16.grad, ...), custom_call_target="tpu_custom_call" | custom-call | tf_op jit(solution)/shard_map/pallas_call | solution.py:467

commit v5 on v4

--- a/solution.py
+++ b/solution.py
@@ -199,10 +199,12 @@
         for h in range(2):
             @pl.when(jnp.logical_not(is_self[h]))
             def _():
-                pltpu.make_async_remote_copy(
-                    src_ref=src.at[pl.ds(16 * h, 16)], dst_ref=dst.at[core], send_sem=send.at[h], recv_sem=recv.at[core],
-                    device_id=opposite[h], device_id_type=MESH,
-                ).start()
+                for k in range(2):
+                    lanes = pl.ds(512 * k, 512)
+                    pltpu.make_async_remote_copy(
+                        src_ref=src.at[pl.ds(16 * h, 16), lanes], dst_ref=dst.at[core, :, lanes], send_sem=send.at[h], recv_sem=recv.at[core],
+                        device_id=opposite[h], device_id_type=MESH,
+                    ).start()
 
             @pl.when(is_self[h])
             def _():
@@ -266,17 +268,17 @@
     branch = conv(hidden_groups, mat_two, 32) + wide_two
     summed[...] = (source + jnp.concatenate([branch[g] for g in range(4)], axis=1)).astype(BF16)
 
+    windows(hidden_groups, 4, 32, hidden_turned)
+    windows(source_groups, 6, 40, source_turned)
+    source_turned[:, 240:QUAD] = jnp.zeros((9 * QUAD, 16), BF16)
+    for h in range(2):
+        pltpu.make_async_copy(mirror.at[h], mirror.at[h], m_recv.at[h]).wait()
     for step in range(1, DEPTH):
         pltpu.make_async_remote_copy(
             src_ref=summed.at[:, pl.ds(128 * step, 128)], dst_ref=relay.at[depth], send_sem=r_send, recv_sem=r_recv,
             device_id=depth_id(row, col, lax.rem(depth + step, DEPTH)), device_id_type=MESH,
         ).start()
     relay[depth] = summed[:, 0:128]
-    windows(hidden_groups, 4, 32, hidden_turned)
-    windows(source_groups, 6, 40, source_turned)
-    source_turned[:, 240:QUAD] = jnp.zeros((9 * QUAD, 16), BF16)
-    for h in range(2):
-        pltpu.make_async_copy(mirror.at[h], mirror.at[h], m_recv.at[h]).wait()
     turned_cot = jnp.concatenate([turned(mirror[h].astype(F32), spare, 256 * h) for h in range(2)], axis=0)
     sym = ((cot[...].astype(F32) + turned_cot) * 0.5).astype(BF16).astype(F32)
 

time: 55.4 us -> 55.1 us (level)
  no operation moved by 1% of the time
where the time goes in v5:
time: 55.1 us; the launch traced here: 55 us
  Pallas kernels  54.4 us (99%)
  between operations  0.64 us (1%)
    pallas_call x1, Pallas kernels, on_device(): pl.pallas_call(kernel, out_shape=(pltpu.VMEM((ROWS, WIDTH), BF16), pltpu....  53.3 us
    pallas_call x1, Pallas kernels, on_device(): pl.pallas_call(unfold, out_shape=(tile, tile, taps, bias, taps, bias), in...  1.1 us

profile of v5, /device:TPU:1, one launch (start us, length us, event | category | flops | bytes accessed | tf_op | source)
XLA Modules:
  0.0 55.0 jit_solution(13044098329643221242)
XLA Ops:
  0.6 53.3 %shard_map.109 = (bf16[32,1024]{1,0:T(8,128)(2,1)S(1)}, bf16[32,1024]{1,0:T(8,128)(2,1)S(1)}, f32[64,10,128]{2,1,0:T(8,128)S(1)}) custom-call(bf16[32,1024]{1,0:T(8,128)(2,1)} %act_hbm.1, bf16[32,1024]{1,0:T(8,128)(2,1)} %cot_hbm.1, bf16[3,3,64,64]{3,2,1,0:T(8,128)(2,1)} %one_hbm.1, bf16[3,3,64,64]{3,2,1,0:T(8,128)(2,1)} %two_hbm.1, f32[1,64]{1,0:T(1,128)} %bitcast.4, ...), custom_call_target="tpu_custom_call" | custom-call | tf_op jit(solution)/shard_map/pallas_call | solution.py:431
  53.9 1.1 %shard_map.110 = (bf16[32,1024]{1,0:T(8,128)(2,1)}, bf16[32,1024]{1,0:T(8,128)(2,1)}, f32[3,3,64,64]{3,2,1,0:T(8,128)}, f32[1,64]{1,0:T(1,128)}, f32[3,3,64,64]{3,2,1,0:T(8,128)}, /*index=5*/f32[1,64]{1,0:T(1,128)}) custom-call(bf16[32,1024]{1,0:T(8,128)(2,1)S(1)} %get-tuple-element.15.sym, bf16[32,1024]{1,0:T(8,128)(2,1)S(1)} %get-tuple-element.16.grad, ...), custom_call_target="tpu_custom_call" | custom-call | tf_op jit(solution)/shard_map/pallas_call | solution.py:469
